TPU v7x, 256 devices: a whole 4x4x8 slice. The times are simulated.
256 devices in a mesh: head: 16 (over z, core), seq: 16 (over y, x).
Axes of the slice: x: 4, y: 4, z: 8, core: 2. Of those that a mesh axis runs over, the one named last changes fastest.
Arguments:
- projected: bfloat16 [32768, 3, 2048], P(('seq', 'head'))
- query_gain: float32 [128], replicated, may hold values from 1.2 to 2
- key_gain: float32 [128], replicated, may hold values from 1.2 to 2
- tile_lists: int32 [16, 256, 96], P('head'), may hold values from 0 to 255, as said below
- tile_counts: int32 [16, 256], P('head'), may hold values from 1 to 96, as said below
Outputs:
- attended: bfloat16 [32768, 2048], P(('seq', 'head'))
Inputs may be any that keep to these rules, and one draw needn't show every extreme that they name: `tile_lists`: for each head and query tile the first tile_counts entries are distinct key tile numbers; later entries are tile numbers that carry no meaning. Tile k lies in frame k * 128 // 2048; a live entry whose frame is more than 4 frames from the query tile's frame is among the first 4 tiles of its frame. tile_counts[h, t] is the number of live entries of tile_lists[h, t]; some query tile of some head has 96 in every draw.
All inputs are finite; a program needn't handle non-finite values.
Results may differ from a plain program's by a relative error of at most 0.012.
The roundings to bfloat16 on the way count: a program that leaves them out, or rounds other values in their place, can miss the bound.
Values may be sent and summed in bfloat16 or wider, within the bound.
A program may use at most 128 MiB of HBM per device.

v0:
```python
import math

import jax
import jax.numpy as jnp
from jax import lax
from jax.sharding import PartitionSpec as P

TILE = 128
GW = 64
GROUP = 4
BATCH = 16


ROPE_THETA = 256.0


def norm_rope(field, gain, positions, frame_tok):
    field = field * lax.rsqrt(jnp.mean(field * field, -1, keepdims=True) + 1e-06) * gain
    head_size = field.shape[-1]
    frame_index = positions // frame_tok
    remainder = positions % frame_tok
    row_index = remainder // GW
    column = remainder % GW
    width_one = head_size // 8
    width_two = (head_size - width_one) // 2
    extents = (width_one, width_two, head_size - width_one - width_two)
    pieces = []
    offset = 0
    for coordinate, extent in zip((frame_index, row_index, column), extents):
        middle = extent // 2
        inverse = ROPE_THETA ** (-2.0 * jnp.arange(middle, dtype=jnp.float32) / extent)
        angles = coordinate.astype(jnp.float32)[:, None] * inverse[None, :]
        leading = field[..., offset : offset + middle]
        trailing = field[..., offset + middle : offset + extent]
        cosine = jnp.cos(angles)
        sines = jnp.sin(angles)
        pieces.append(leading * cosine - trailing * sines)
        pieces.append(trailing * cosine + leading * sines)
        offset = offset + extent
    return jnp.concatenate(pieces, -1)


def attend(query_tiles, lists_here, counts_here, end_item, key_blocks, value_blocks):
    tile_total = query_tiles.shape[0]
    tile_size = query_tiles.shape[1]
    head_size = query_tiles.shape[2]
    per_tile = (counts_here + GROUP - 1) // GROUP
    item_ends = jnp.cumsum(per_tile)
    item_starts = item_ends - per_tile
    tile_index = jnp.arange(tile_total, dtype=jnp.int32)
    slot_index = jnp.arange(lists_here.shape[1], dtype=jnp.int32)
    in_group = jnp.arange(GROUP, dtype=jnp.int32)
    factor = 1.0 / math.sqrt(head_size)

    def one_turn(turn_index, running):
        numerator, denominator = running
        item_ids = turn_index * BATCH + jnp.arange(BATCH, dtype=jnp.int32)
        is_live = item_ids < end_item
        owner_tile = jnp.minimum(
            jnp.sum((item_ids[:, None] >= item_ends[None, :]).astype(jnp.int32), 1), tile_total - 1
        )
        owner_mask = owner_tile[:, None] == tile_index[None, :]
        first_slot = jnp.sum(jnp.where(owner_mask, item_starts[None, :], 0), 1)
        slot_ids = (item_ids - first_slot)[:, None] * GROUP + in_group[None, :]
        row_lists = jnp.sum(jnp.where(owner_mask[:, :, None], lists_here[None, :, :], 0), 1)
        row_counts = jnp.sum(jnp.where(owner_mask, counts_here[None, :], 0), 1)
        chosen = jnp.sum(
            jnp.where(slot_ids[:, :, None] == slot_index[None, None, :], row_lists[:, None, :], 0),
            2,
        )
        slot_valid = (slot_ids < row_counts[:, None]) & is_live[:, None]
        batched_keys = key_blocks[chosen].reshape(BATCH, GROUP * tile_size, head_size)
        batched_values = value_blocks[chosen].reshape(BATCH, GROUP * tile_size, head_size)
        batched_queries = query_tiles[owner_tile]
        scores = (
            jnp.einsum(
                "trl,tvl->trv", batched_queries, batched_keys, preferred_element_type=jnp.float32
            )
            * factor
        )
        key_valid = jnp.repeat(slot_valid, tile_size, axis=1)
        weights = jnp.where(key_valid[:, None, :], jnp.exp(scores), 0.0)
        batch_denom = jnp.sum(weights, 2)
        batch_numerator_sum = jnp.einsum(
            "ysu,yuw->ysw",
            weights.astype(jnp.bfloat16),
            batched_values,
            preferred_element_type=jnp.float32,
        )
        owner_portion = owner_mask.astype(jnp.float32)
        numerator = numerator + jnp.einsum(
            "vf,vpk->fpk", owner_portion, batch_numerator_sum, precision=lax.Precision.HIGHEST
        )
        denominator = denominator + jnp.einsum(
            "bn,bq->nq", owner_portion, batch_denom, precision=lax.Precision.HIGHEST
        )
        return (numerator, denominator)

    turn_total = (end_item + BATCH - 1) // BATCH
    initial = (
        jnp.zeros((tile_total, tile_size, head_size), jnp.float32),
        jnp.zeros((tile_total, tile_size), jnp.float32),
    )
    return lax.fori_loop(0, turn_total, one_turn, initial)


def local(projected, query_gain, key_gain, tile_lists, tile_counts):
    tok_dev = projected.shape[0]
    head_size = query_gain.shape[0]
    head_count = projected.shape[2] // head_size
    own_rows = projected.reshape(tok_dev, 3, head_count, head_size)
    by_head = lax.all_to_all(own_rows, "head", split_axis=2, concat_axis=0, tiled=True)
    seq_tok = by_head.shape[0]
    seq_index = lax.axis_index("seq")
    positions = seq_index * seq_tok + jnp.arange(seq_tok, dtype=jnp.int32)
    queries = norm_rope(
        by_head[:, 0, 0].astype(jnp.float32), query_gain, positions, seq_tok
    ).astype(jnp.bfloat16)
    key_rows = norm_rope(by_head[:, 1, 0].astype(jnp.float32), key_gain, positions, seq_tok).astype(
        jnp.bfloat16
    )
    value_rows = by_head[:, 2, 0]
    own_tiles = seq_tok // TILE
    head_lists = tile_lists[0]
    head_counts = tile_counts[0]
    own_lists = lax.dynamic_slice_in_dim(head_lists, seq_index * own_tiles, own_tiles, 0)
    own_counts = lax.dynamic_slice_in_dim(head_counts, seq_index * own_tiles, own_tiles, 0)
    all_keys, all_values = (
        lax.all_gather(key_rows, "seq", axis=0, tiled=True),
        lax.all_gather(value_rows, "seq", axis=0, tiled=True),
    )
    key_blocks = all_keys.reshape(-1, TILE, head_size)
    value_blocks = all_values.reshape(-1, TILE, head_size)
    own_queries = queries.reshape(own_tiles, TILE, head_size)
    item_total = jnp.sum((own_counts + GROUP - 1) // GROUP)
    numerator, denominator = attend(
        own_queries, own_lists, own_counts, item_total, key_blocks, value_blocks
    )
    normalized = (
        (numerator / denominator[..., None]).astype(jnp.bfloat16).reshape(seq_tok, 1, head_size)
    )
    by_token = lax.all_to_all(normalized, "head", split_axis=0, concat_axis=1, tiled=True)
    return by_token.reshape(tok_dev, head_count * head_size)


def solution(mesh):
    in_specs = (P(("seq", "head"), None, None), P(), P(), P("head", None, None), P("head", None))
    out_specs = P(("seq", "head"), None)
    return jax.shard_map(local, mesh=mesh, in_specs=in_specs, out_specs=out_specs, check_vma=False)
```

profile of v0, /device:TPU:5, one launch (start us, length us, event | category | flops | bytes accessed | tf_op | source)
XLA Modules:
  0.0 685.8 jit_solution(4337063495499491849)
XLA Ops:
  10.1 9.2 %all-to-all-start = ((bf16[128,3,16,128]{3,0,1,2:T(8,128)(2,1)}), bf16[128,3,16,128]{3,0,1,2:T(8,128)(2,1)S(1)}, u32[]{:S(2)}, u32[]{:S(2)}) async-start(bf16[128,3,16,128]{3,0,1,2:T(8,128)(2,1)} %copy.69), calls=%async_computation | async-start | bytes 3145728 | tf_op jit(solution)/shard_map/all_to_all | solution.py:112
  19.4 38.3 %all-to-all-done = bf16[128,3,16,128]{3,0,1,2:T(8,128)(2,1)S(1)} async-done(((bf16[128,3,16,128]{3,0,1,2:T(8,128)(2,1)}), bf16[128,3,16,128]{3,0,1,2:T(8,128)(2,1)S(1)}, u32[]{:S(2)}, u32[]{:S(2)}) %all-to-all-start) | async-done | bytes 1572896 | tf_op jit(solution)/shard_map/all_to_all | solution.py:112
  62.7 5.6 concatenate.28
  76.3 65.9 %all-gather.4.cloned.1.call-done = bf16[32768,128]{0,1:T(8,128)(2,1)} async-done(((bf16[2048,128]{0,1:T(8,128)(2,1)}), bf16[32768,128]{0,1:T(8,128)(2,1)}) %all-gather.4.cloned.1.call-update) | async-done | bytes 8388624 | tf_op jit(solution)/shard_map/all_gather | solution.py:129
  142.2 11.9 %copy.89 = bf16[32768,128]{1,0:T(8,128)(2,1)} copy(bf16[32768,128]{0,1:T(8,128)(2,1)} %all-gather.4.cloned.1.call-done) | data formatting | bytes 16777216
  154.0 66.1 %all-gather.6.cloned.1.call-done = bf16[32768,1,1,128]{3,0,1,2:T(8,128)(2,1)} async-done(((bf16[2048,1,1,128]{3,0,1,2:T(8,128)(2,1)}), bf16[32768,1,1,128]{3,0,1,2:T(8,128)(2,1)}) %all-gather.6.cloned.1.call-update) | async-done | bytes 8388624 | tf_op jit(solution)/shard_map/all_gather | solution.py:130
  221.2 390.9 %while.13 = (s32[]{:T(128)}, f32[16,128,128]{2,0,1:T(8,128)}, f32[16,128]{1,0:T(8,128)S(1)}, s32[]{:T(128)}, s32[16]{0:T(128)S(1)}, /*index=5*/s32[16]{0:T(128)S...) while((s32[]{:T(128)}, f32[16,128,128]{2,0,1:T(8,128)}, ...), condition=%wide.region_11.12_spmd.clone, body=%wide.region_4.11_spmd.clone.sunk | while | flops 594220800 | bytes 39428080 | solution.py:104
  223.0 4.3 gather_fusion.2
  242.5 4.3 gather_fusion.2
  262.1 4.3 gather_fusion.2
  281.6 4.3 gather_fusion.2
  301.1 4.3 gather_fusion.2
  320.7 4.3 gather_fusion.2
  340.2 4.3 gather_fusion.2
  359.8 4.3 gather_fusion.2
  379.3 4.3 gather_fusion.2
  398.9 4.3 gather_fusion.2
  418.4 4.3 gather_fusion.2
  438.0 4.3 gather_fusion.2
  457.5 4.3 gather_fusion.2
  477.1 4.3 gather_fusion.2
  555.2 4.3 gather_fusion.2
  574.8 4.3 gather_fusion.2
  615.4 61.6 %all_to_all.33 = bf16[16,2,8192]{2,1,0:T(2,128)(2,1)S(1)} all-to-all(bf16[16,2,8192]{2,1,0:T(2,128)(2,1)S(1)} %reshape.366), channel_id=1, replica_groups=mesh['head'=16,'seq'=16] {'head'}, dimensions={0} | all-to-all | bytes 1048576 | tf_op jit(solution)/shard_map/all_to_all | solution.py:142
  (758 shorter events, 340.5 us)
Async XLA Ops:
  6.5 64.2 %copy-start = (s32[1,256,96]{1,2,0:T(8,128)S(1)}, s32[1,256,96]{1,2,0:T(8,128)}, u32[]{:S(2)}) copy-start(s32[1,256,96]{1,2,0:T(8,128)} %param.10) | copy-start | bytes 294916
  10.1 47.6 %all-to-all-start = ((bf16[128,3,16,128]{3,0,1,2:T(8,128)(2,1)}), bf16[128,3,16,128]{3,0,1,2:T(8,128)(2,1)S(1)}, u32[]{:S(2)}, u32[]{:S(2)}) async-start(bf16[128,3,16,128]{3,0,1,2:T(8,128)(2,1)} %copy.69), calls=%async_computation | async-start | bytes 3145728 | tf_op jit(solution)/shard_map/all_to_all | solution.py:112
  19.2 122.9 %all-gather.4.cloned.1.call-start = ((), (), s32[]{:S(2)}) async-start(), calls=%async_computation.2 | async-start | bytes 8912896 | tf_op jit(solution)/shard_map/all_gather | solution.py:129
  60.1 8.9 %copy-start.7 = (s32[1,256]{1,0:T(1,128)S(1)}, s32[1,256]{1,0:T(1,128)}, u32[]{:S(2)}) copy-start(s32[1,256]{1,0:T(1,128)} %param.11) | copy-start | bytes 3076
  68.2 151.9 %all-gather.6.cloned.1.call-start = ((), (), s32[]{:S(2)}) async-start(), calls=%async_computation.3 | async-start | bytes 8912896 | tf_op jit(solution)/shard_map/all_gather | solution.py:130
  240.7 6.2 copy-start.3
  260.3 6.2 copy-start.3
  279.8 6.2 copy-start.3
  299.3 6.2 copy-start.3
  318.9 6.2 copy-start.3
  338.4 6.2 copy-start.3
  358.0 6.2 copy-start.3
  377.5 6.2 copy-start.3
  397.1 6.2 copy-start.3
  416.6 6.2 copy-start.3
  436.2 6.2 copy-start.3
  455.7 6.2 copy-start.3
  475.2 6.2 copy-start.3
  494.8 6.2 copy-start.3
  514.3 6.2 copy-start.3
  533.9 6.2 copy-start.3
  553.4 6.2 copy-start.3
  573.0 6.2 copy-start.3
  592.5 6.2 copy-start.3
  (63 other events, 138.5 us)
Sparse Core Ops, SparseCore 0:
  68.4 73.7 all-gather.3
  144.6 75.4 all-gather.5
where the time goes:
time: 688 us; the launch traced here: 686 us
  local copies, waits for them, and re-layouts  244 us (35%)
  waiting for transfers between devices  171 us (25%)
  matrix products  149 us (22%)
  blocking collectives  61.6 us (9%)
  other arithmetic  33 us (5%)
  between operations  14.3 us (2%)
  starting transfers between devices  9.23 us (1%)
    gather x20, local copies, waits for them, and re-layouts, one_turn(): key_blocks[chosen].reshape(BATCH, GROUP * tile_size, head_size)  86.6 us
    gather x20, local copies, waits for them, and re-layouts, one_turn(): value_blocks[chosen].reshape(BATCH, GROUP * tile_size, head_size)  86.6 us
    all_gather x1, waiting for transfers between devices, local(): lax.all_gather(value_rows, 'seq', axis=0, tiled=True)  66.1 us
    all_gather x1, waiting for transfers between devices, local(): lax.all_gather(key_rows, 'seq', axis=0, tiled=True)  65.9 us
    all_to_all x1, blocking collectives, local(): lax.all_to_all(normalized, 'head', split_axis=0, concat_axis=1, tiled=True)  61.6 us
    dot_general x20, matrix products, one_turn(): jnp.einsum('ysu,yuw->ysw', weights.astype(jnp.bfloat16), batched_values,...  61.2 us
    dot_general x20, matrix products, one_turn(): jnp.einsum('trl,tvl->trv', batched_queries, batched_keys, preferred_eleme...  56.3 us
    all_to_all x1, waiting for transfers between devices, local(): lax.all_to_all(own_rows, 'head', split_axis=2, concat_axis=0, tiled=True)  38.3 us
  transfers between devices with their start and end apart: 3, of which 3 were waited for; matrix products, arithmetic and copies ran while one was open for 3% of the time, Pallas kernels for 0%

commit v1 on v0

v1 whole, which is shorter than its diff:
```python
import functools
import math

import jax
import jax.numpy as jnp
from jax import lax
from jax.experimental import pallas as pl
from jax.experimental.pallas import tpu as pltpu
from jax.sharding import PartitionSpec as P


TILE = 128
HD = 128
GW = 64
HEADS = 16
FRAMES = 16
PER = 16
CH = 4
PAIRS = 8
THETA = 256.0
SCALE = math.log2(math.e) / math.sqrt(HD)
G = 8
SUB = 2
MESH = pl.DeviceIdType.MESH
f32 = jnp.float32
bf16 = jnp.bfloat16


def rope_tables(sq, hd):
    tokens = hd * TILE + jnp.arange(TILE, dtype=jnp.int32)
    row = tokens // GW
    column = tokens % GW
    frame = jnp.full((TILE,), sq, jnp.int32)
    first = HD // 8
    second = (HD - first) // 2
    cosines, sines = [], []
    for coordinate, extent in zip((frame, row, column), (first, second, HD - first - second)):
        middle = extent // 2
        inverse = THETA ** (-2.0 * jnp.arange(middle, dtype=f32) / extent)
        angles = coordinate.astype(f32)[:, None] * inverse[None, :]
        c, s = jnp.cos(angles), jnp.sin(angles)
        cosines += [c, c]
        sines += [-s, s]
    return jnp.concatenate(cosines, 1), jnp.concatenate(sines, 1)


def partner(field):
    lane = lax.broadcasted_iota(jnp.int32, field.shape, 1)
    first = HD // 8
    half = (HD - first) // 4
    near = jnp.where(lane < first // 2, pltpu.roll(field, HD - first // 2, 1), pltpu.roll(field, first // 2, 1))
    offset = lane - first
    lower = (offset < half) | ((offset >= 2 * half) & (offset < 3 * half))
    far = jnp.where(lower, pltpu.roll(field, HD - half, 1), pltpu.roll(field, half, 1))
    return jnp.where(lane < first, near, far)


def prepare_kernel(proj, cos, sin, qg, kg, q_out, kv_out):
    cosine = cos[...]
    sine = sin[...]
    for h in range(HEADS):
        for part, gain in ((0, qg), (1, kg)):
            lo = (part * HEADS + h) * HD
            field = proj[:, lo:lo + HD].astype(f32)
            mean = jnp.sum(field * field, axis=1, keepdims=True) * (1.0 / HD)
            field = field * lax.rsqrt(mean + 1e-06) * gain[...]
            turned = (field * cosine + partner(field) * sine).astype(bf16)
            if part == 0:
                q_out[h] = turned
            else:
                kv_out[h, 0] = turned
        lo = (2 * HEADS + h) * HD
        kv_out[h, 1] = proj[:, lo:lo + HD]


def place():
    hd = lax.axis_index("head")
    sq = lax.axis_index("seq")
    z, c = hd // 2, hd % 2
    y, x = sq // 4, sq % 4
    b, k = x // 2, x % 2
    return hd, sq, z, c, y, x, b, k


def spread_kernel(q_in, kv_in, lists_in, counts_in, q, kv, lists, counts,
                  s1kv, s1q, r1kv, r1q, s2, r2, s3, r3, sl, rl):
    hd, sq, z, c, y, x, b, k = place()
    p = 2 * y + k
    frame = 2 * p + c

    def dev(h, s):
        return {"head": h, "seq": s}

    def pair_dev(pt):
        return dev(hd, 4 * (pt // 2) + 2 * b + pt % 2)

    sibling = dev(2 * z + 1 - c, sq)

    def home(r, bb):
        zt = (z + r) % 8
        return zt, 2 * zt + x % 2, 4 * y + 2 * bb + x // 2

    barrier = pltpu.get_barrier_semaphore()
    for t in range(HEADS):
        @pl.when((t != hd) | (frame != sq))
        def _():
            pl.semaphore_signal(barrier, 1, device_id=dev(t, frame), device_id_type=MESH)
    for d in range(1, PAIRS):
        pl.semaphore_signal(barrier, 1, device_id=pair_dev((p + d) % PAIRS), device_id_type=MESH)
    pl.semaphore_signal(barrier, 1, device_id=sibling, device_id_type=MESH)
    self_home = (frame == sq).astype(jnp.int32)
    pl.semaphore_wait(barrier, HEADS - self_home + PAIRS)

    def phase1(src, dst, send, recv, r, bb, act):
        zt, ht, st = home(r, bb)
        head = 2 * zt + bb
        remote = (ht != hd) | (st != sq)

        @pl.when(remote)
        def _():
            cp = pltpu.make_async_remote_copy(src.at[head], dst, send.at[r * 2 + bb], recv.at[hd],
                                              device_id=dev(ht, st), device_id_type=MESH)
            cp.start() if act else cp.wait_send()

        if act:
            @pl.when(jnp.logical_not(remote))
            def _():
                pltpu.make_async_copy(src.at[head], dst, recv.at[hd]).start()

    kv_home = kv.at[sq * PER + hd]
    q_home = q.at[hd]
    for r in range(8):
        for bb in range(2):
            phase1(kv_in, kv_home, s1kv, r1kv, r, bb, True)
    for r in range(8):
        for bb in range(2):
            phase1(q_in, q_home, s1q, r1q, r, bb, True)

    def list_copies(rows, device):
        return (pltpu.make_async_remote_copy(lists_in.at[pl.ds(rows * PER, PER)], lists, sl.at[0], rl.at[0],
                                             device_id=device, device_id_type=MESH),
                pltpu.make_async_remote_copy(counts_in, counts, sl.at[1], rl.at[1],
                                             device_id=device, device_id_type=MESH))

    @pl.when(b == c)
    def _():
        for cp in list_copies(4 * y + 2 * k + 1 - c, sibling):
            cp.start()
        pltpu.make_async_copy(lists_in.at[pl.ds(frame * PER, PER)], lists, rl.at[0]).start()
        pltpu.make_async_copy(counts_in, counts, rl.at[1]).start()

    def span(fr, m):
        return kv.at[pl.ds(fr * PER + m * CH, CH)]

    def lane_copy(d, m):
        part = span(frame, m)
        return pltpu.make_async_remote_copy(part, part, s2.at[d + PAIRS - 1, m], r2.at[p, m],
                                            device_id=pair_dev(p + d), device_id_type=MESH)

    def lane_arrival(pt, m):
        part = span(2 * pt + c, m)
        return pltpu.make_async_remote_copy(part, part, s2.at[0, 0], r2.at[pt, m],
                                            device_id=sibling, device_id_type=MESH)

    def cross_copy(pt, m, core):
        part = span(2 * pt + core, m)
        return pltpu.make_async_remote_copy(part, part, s3.at[pt, m], r3.at[pt, m],
                                            device_id=sibling, device_id_type=MESH)

    def inside(pt):
        return (pt >= 0) & (pt < PAIRS)

    def crosses(dp, m, core):
        if abs(dp) <= 1:
            return True
        if dp == 2:
            return (core == 0) | (m == 0)
        if dp == -2:
            return (core == 1) | (m == 0)
        return m == 0

    def own(m):
        for t in range(CH):
            j = m * CH + t
            pltpu.make_async_copy(kv.at[frame * PER + j], kv.at[frame * PER + j], r1kv.at[j]).wait()
        for d in (1, -1, 2, -2):
            @pl.when(inside(p + d))
            def _():
                lane_copy(d, m).start()
        cross_copy(p, m, c).start()
        for d in range(3, PAIRS):
            for sgn in (1, -1):
                @pl.when(inside(p + sgn * d) & (m == 0))
                def _():
                    lane_copy(sgn * d, m).start()

    def relay(m):
        for d in (1, -1, 2, -2):
            pt = p + d

            @pl.when(inside(pt))
            def _():
                lane_arrival(pt, m).wait_recv()

            @pl.when(inside(pt) & crosses(d, m, c))
            def _():
                cross_copy(pt, m, c).start()
        for d in range(3, PAIRS):
            for sgn in (1, -1):
                pt = p + sgn * d

                @pl.when(inside(pt) & (m == 0))
                def _():
                    lane_arrival(pt, m).wait_recv()
                    cross_copy(pt, m, c).start()

    order = [(z // 2 + 4 - i) % 4 for i in range(4)]
    own(order[0])
    own(order[1])
    relay(order[0])
    own(order[2])
    relay(order[1])
    own(order[3])
    relay(order[2])
    relay(order[3])

    for j in range(PER):
        pltpu.make_async_copy(q.at[j], q.at[j], r1q.at[j]).wait()
    pltpu.make_async_copy(lists_in.at[pl.ds(frame * PER, PER)], lists, rl.at[0]).wait()
    pltpu.make_async_copy(counts_in, counts, rl.at[1]).wait()

    @pl.when(b == c)
    def _():
        for cp in list_copies(4 * y + 2 * k + 1 - c, sibling):
            cp.wait_send()

    for m in range(4):
        for d in range(1 - PAIRS, PAIRS):
            if d != 0 and (abs(d) <= 2 or m == 0):
                @pl.when(inside(p + d))
                def _():
                    lane_copy(d, m).wait_send()
            if abs(d) <= 2 or m == 0:
                @pl.when(inside(p + d) & crosses(d, m, c))
                def _():
                    cross_copy(p + d, m, c).wait_send()

                @pl.when(inside(p + d) & crosses(d, m, 1 - c))
                def _():
                    cross_copy(p + d, m, 1 - c).wait_recv()
    for r in range(8):
        for bb in range(2):
            phase1(kv_in, kv_home, s1kv, r1kv, r, bb, False)
            phase1(q_in, q_home, s1q, r1q, r, bb, False)


def attend_kernel(lists, counts, q_ref, kv_hbm, o_ref, kv, s0, s1, acc, den, sems):
    _, _, _, c, y, _, _, k = place()
    frame = 4 * y + 2 * k + c

    def loads(act):
        for fr in range(FRAMES):
            near = jnp.abs(fr - frame) <= 4

            @pl.when(near)
            def _():
                part = pl.ds(fr * PER, PER)
                act(pltpu.make_async_copy(kv_hbm.at[part], kv.at[part], sems.at[fr]))

            @pl.when(jnp.logical_not(near))
            def _():
                part = pl.ds(fr * PER, CH)
                act(pltpu.make_async_copy(kv_hbm.at[part], kv.at[part], sems.at[fr]))

    loads(lambda cp: cp.start())
    acc[...] = jnp.zeros_like(acc)
    den[...] = jnp.zeros_like(den)

    def count(i):
        return counts[0, frame * PER + i]

    total = lax.fori_loop(0, PER, lambda i, t: t + (count(i) + G - 1) // G, 0)
    loads(lambda cp: cp.wait())

    def following(i, g):
        stay = ((g + 1) * G < count(i)) | (i == PER - 1)
        return jnp.where(stay, i, i + 1), jnp.where(stay, g + 1, 0)

    def ids(i, g):
        last = count(i) - 1
        return [lists[i, jnp.minimum(g * G + u, last)] for u in range(G)]

    def score(i, g, s):
        chosen = ids(i, g)
        q = q_ref[i]
        for w in range(0, G, SUB):
            keys = jnp.concatenate([kv[t, 0] for t in chosen[w:w + SUB]], 0)
            s[:, w * TILE:(w + SUB) * TILE] = lax.dot_general(
                q, keys, (((1,), (1,)), ((), ())), preferred_element_type=f32)

    def weigh(i, g, s):
        chosen = ids(i, g)
        n = count(i)
        d = jnp.zeros((TILE, TILE), f32)
        a = jnp.zeros((TILE, HD), f32)
        for w in range(0, G, SUB):
            e = jnp.exp2(s[:, w * TILE:(w + SUB) * TILE] * SCALE)
            parts = [jnp.where(g * G + w + u < n, e[:, u * TILE:(u + 1) * TILE], 0.0) for u in range(SUB)]
            for part in parts:
                d = d + part
            weights = jnp.concatenate(parts, 1).astype(bf16)
            values = jnp.concatenate([kv[t, 1] for t in chosen[w:w + SUB]], 0)
            a = a + lax.dot_general(weights, values, (((1,), (0,)), ((), ())), preferred_element_type=f32)
        acc[i] += a
        den[i] += d

    zero = jnp.int32(0)
    score(zero, zero, s0)

    def body(_, state):
        i, g = state
        i1, g1 = following(i, g)
        score(i1, g1, s1)
        weigh(i, g, s0)
        i2, g2 = following(i1, g1)
        score(i2, g2, s0)
        weigh(i1, g1, s1)
        return i2, g2

    lax.fori_loop(0, (total + 1) // 2, body, (zero, zero))

    def finish(i, _):
        o_ref[i] = (acc[i] / jnp.sum(den[i], axis=1, keepdims=True)).astype(bf16)
        return 0

    lax.fori_loop(0, PER, finish, 0)


def return_kernel(o_in, out, send, recv):
    hd, sq, z, c, y, x, b, k = place()
    frame = 4 * y + 2 * k + c
    head = 2 * z + b
    barrier = pltpu.get_barrier_semaphore()

    def source(h):
        return 2 * (h // 2) + x % 2, 4 * y + 2 * (h % 2) + x // 2

    self_home = (frame == sq).astype(jnp.int32)
    for h in range(HEADS):
        hs, ss = source(h)

        @pl.when((hs != hd) | (ss != sq))
        def _():
            pl.semaphore_signal(barrier, 1, device_id={"head": hs, "seq": ss}, device_id_type=MESH)
    pl.semaphore_wait(barrier, HEADS - self_home)
    columns = out.at[:, pl.ds(pl.multiple_of(head * HD, HD), HD)]

    def copies(act):
        for r in range(HEADS):
            t = (hd + r) % HEADS
            remote = (t != hd) | (frame != sq)

            @pl.when(remote)
            def _():
                cp = pltpu.make_async_remote_copy(o_in.at[t], columns, send.at[r], recv.at[head],
                                                  device_id={"head": t, "seq": frame}, device_id_type=MESH)
                cp.start() if act else cp.wait_send()

            if act:
                @pl.when(jnp.logical_not(remote))
                def _():
                    pltpu.make_async_copy(o_in.at[t], columns, recv.at[head]).start()

    copies(True)
    for h in range(HEADS):
        part = out.at[:, pl.ds(h * HD, HD)]
        pltpu.make_async_copy(o_in.at[0], part, recv.at[h]).wait()
    copies(False)


def local(projected, query_gain, key_gain, tile_lists, tile_counts):
    hd = lax.axis_index("head")
    sq = lax.axis_index("seq")
    vmem = pl.BlockSpec(memory_space=pltpu.VMEM)
    smem = pl.BlockSpec(memory_space=pltpu.SMEM)
    hbm = pl.BlockSpec(memory_space=pl.ANY)
    sds = jax.ShapeDtypeStruct
    dma = pltpu.SemaphoreType.DMA
    cosine, sine = rope_tables(sq, hd)
    q_own, kv_own = pl.pallas_call(
        prepare_kernel,
        out_shape=(sds((HEADS, TILE, HD), bf16), sds((HEADS, 2, TILE, HD), bf16)),
        in_specs=[vmem] * 5,
        out_specs=(vmem, vmem),
        name="prepare",
    )(projected.reshape(TILE, 3 * HEADS * HD), cosine, sine, query_gain[None], key_gain[None])
    q, kv, lists, counts = pl.pallas_call(
        spread_kernel,
        out_shape=(sds((PER, TILE, HD), bf16), sds((FRAMES * PER, 2, TILE, HD), bf16),
                   sds((PER, 96), jnp.int32), sds((1, FRAMES * PER), jnp.int32)),
        in_specs=[hbm] * 4,
        out_specs=(hbm,) * 4,
        scratch_shapes=[dma((16,)), dma((16,)), dma((16,)), dma((16,)), dma((2 * PAIRS - 1, 4)), dma((PAIRS, 4)),
                        dma((PAIRS, 4)), dma((PAIRS, 4)), dma((2,)), dma((2,))],
        compiler_params=pltpu.CompilerParams(collective_id=0, has_side_effects=True),
        name="spread",
    )(q_own, kv_own, tile_lists[0], tile_counts)
    attended = pl.pallas_call(
        attend_kernel,
        out_shape=sds((PER, TILE, HD), bf16),
        in_specs=[smem, smem, vmem, hbm],
        out_specs=vmem,
        scratch_shapes=[pltpu.VMEM((FRAMES * PER, 2, TILE, HD), bf16), pltpu.VMEM((TILE, G * TILE), f32),
                        pltpu.VMEM((TILE, G * TILE), f32), pltpu.VMEM((PER, TILE, TILE), f32),
                        pltpu.VMEM((PER, TILE, HD), f32), dma((FRAMES,))],
        compiler_params=pltpu.CompilerParams(vmem_limit_bytes=40 * 1024 * 1024),
        name="attend",
    )(lists, counts, q, kv)
    return pl.pallas_call(
        return_kernel,
        out_shape=sds((TILE, HEADS * HD), bf16),
        in_specs=[hbm],
        out_specs=hbm,
        scratch_shapes=[dma((HEADS,)), dma((HEADS,))],
        compiler_params=pltpu.CompilerParams(collective_id=1, has_side_effects=True),
        name="give_back",
    )(attended)


def solution(mesh):
    in_specs = (P(("seq", "head"), None, None), P(), P(), P("head", None, None), P("head", None))
    return jax.shard_map(local, mesh=mesh, in_specs=in_specs, out_specs=P(("seq", "head"), None), check_vma=False)
```

time: 688 us -> 190 us (0.28)
  the two profiles are of different devices: /device:TPU:5 before, /device:TPU:17 now
where the time goes in v1:
time: 190 us
  Pallas kernels  178 us (94%)
  local copies, waits for them, and re-layouts  10.9 us (6%)
    pallas_call x1, Pallas kernels, local(): pl.pallas_call(spread_kernel, out_shape=(sds((PER, TILE, HD), bf16), sds(...  110 us
    pallas_call x1, Pallas kernels, local(): pl.pallas_call(attend_kernel, out_shape=sds((PER, TILE, HD), bf16), in_sp...  43 us
    pallas_call x1, Pallas kernels, local(): pl.pallas_call(return_kernel, out_shape=sds((TILE, HEADS * HD), bf16), in...  17.4 us
    pallas_call x1, Pallas kernels, local(): pl.pallas_call(prepare_kernel, out_shape=(sds((HEADS, TILE, HD), bf16), s...  7.97 us
    unnamed x13, local copies, waits for them, and re-layouts  7.7 us

profile of v1, /device:TPU:17, one launch (start us, length us, event | category | flops | bytes accessed | tf_op | source)
XLA Modules:
  0.0 190.1 jit_solution(541531688874149145)
XLA Ops:
  0.0 0.0 copy-start.4
  0.0 0.1 fusion.6
  0.1 0.1 fusion.4
  0.2 1.7 copy.15
  1.9 0.5 multiply_sine_fusion
  2.5 0.8 concatenate.6.cos
  3.3 0.8 concatenate.7.sin
  4.0 0.0 copy-done.4
  4.0 0.9 copy.11
  4.9 1.6 copy.14.proj
  6.5 8.0 %prepare.1 = (bf16[16,128,128]{2,1,0:T(8,128)(2,1)}, bf16[16,2,128,128]{3,2,1,0:T(8,128)(2,1)}) custom-call(bf16[128,6144]{1,0:T(8,128)(2,1)} %copy.14.proj, f32[128,128]{1,0:T(8,128)} %concatenate.6.cos, f32[128,128]{1,0:T(8,128)} %concatenate.7.sin, f32[1,128]{1,0:T(1,128)} %bitcast.6, f32[1,128]{1,0:T(1,128)} %bitcast.7), custom_call_target="tpu_custom_call" | custom-call | tf_op jit(solution)/shard_map/prepare/pallas_call | solution.py:390
  14.5 110.0 %spread.1 = (bf16[16,128,128]{2,1,0:T(8,128)(2,1)}, bf16[256,2,128,128]{3,2,1,0:T(8,128)(2,1)}, s32[16,96]{1,0:T(8,128)}, s32[1,256]{1,0:T(1,128)}) custom-call(bf16[16,128,128]{2,1,0:T(8,128)(2,1)} %get-tuple-element.11.q_in, bf16[16,2,128,128]{3,2,1,0:T(8,128)(2,1)} %get-tuple-element.12.kv_in, s32[256,96]{1,0:T(8,128)} %bitcast.5, s32[1,256]{1,0:T(1,128)} %counts_in.1), custom_call_target="tpu_custom_call" | custom-call | tf_op jit(solution)/shard_map/spread/pallas_call | solution.py:397
  124.5 0.0 copy-start.1
  124.5 1.0 copy-done.1
  125.5 0.0 copy-start.2
  125.5 0.7 copy-done.2
  126.2 0.0 copy-start.3
  126.2 0.7 copy-done.3
  126.9 43.0 %attend.1.o_in = bf16[16,128,128]{2,1,0:T(8,128)(2,1)S(1)} custom-call(s32[16,96]{1,0:T(8,128)S(1)} %copy-done.2, s32[1,256]{1,0:T(1,128)S(1)} %copy-done.3, bf16[16,128,128]{2,1,0:T(8,128)(2,1)S(1)} %copy-done.1, bf16[256,2,128,128]{3,2,1,0:T(8,128)(2,1)} %get-tuple-element.16.kv_hbm), custom_call_target="tpu_custom_call" | custom-call | tf_op jit(solution)/shard_map/attend/pallas_call | solution.py:408
  169.9 0.0 copy-start
  169.9 0.8 copy-done
  170.7 17.4 %give_back.1 = bf16[128,2048]{1,0:T(8,128)(2,1)} custom-call(bf16[16,128,128]{2,1,0:T(8,128)(2,1)} %copy-done), custom_call_target="tpu_custom_call" | custom-call | tf_op jit(solution)/shard_map/give_back/pallas_call | solution.py:419
  188.2 1.9 copy.17
  (5 shorter events, 0.0 us)
Async XLA Ops:
  0.0 4.0 %copy-start.4 = (bf16[128,3,2048]{2,0,1:T(8,128)(2,1)S(1)}, bf16[128,3,2048]{2,0,1:T(8,128)(2,1)}, u32[]{:S(2)}) copy-start(bf16[128,3,2048]{2,0,1:T(8,128)(2,1)} %param.5) | copy-start | bytes 4718596
  124.5 1.0 copy-start.1
  125.5 0.7 copy-start.2
  126.2 0.7 copy-start.3
  169.9 0.8 copy-start

commit v2 on v1

--- a/solution.py
+++ b/solution.py
@@ -16,11 +16,11 @@
 FRAMES = 16
 PER = 16
 CH = 4
-PAIRS = 8
 THETA = 256.0
 SCALE = math.log2(math.e) / math.sqrt(HD)
 G = 8
 SUB = 2
+HOPS = (0, 1, -1, 2, -2, 3, -3, 4)
 MESH = pl.DeviceIdType.MESH
 f32 = jnp.float32
 bf16 = jnp.bfloat16
@@ -60,8 +60,8 @@
     sine = sin[...]
     for h in range(HEADS):
         for part, gain in ((0, qg), (1, kg)):
-            lo = (part * HEADS + h) * HD
-            field = proj[:, lo:lo + HD].astype(f32)
+            lo = h * HD
+            field = proj[part, :, lo:lo + HD].astype(f32)
             mean = jnp.sum(field * field, axis=1, keepdims=True) * (1.0 / HD)
             field = field * lax.rsqrt(mean + 1e-06) * gain[...]
             turned = (field * cosine + partner(field) * sine).astype(bf16)
@@ -69,8 +69,7 @@
                 q_out[h] = turned
             else:
                 kv_out[h, 0] = turned
-        lo = (2 * HEADS + h) * HD
-        kv_out[h, 1] = proj[:, lo:lo + HD]
+        kv_out[h, 1] = proj[2, :, h * HD:(h + 1) * HD]
 
 
 def place():
@@ -82,176 +81,184 @@
     return hd, sq, z, c, y, x, b, k
 
 
-def spread_kernel(q_in, kv_in, lists_in, counts_in, q, kv, lists, counts,
-                  s1kv, s1q, r1kv, r1q, s2, r2, s3, r3, sl, rl):
+def spread_kernel(q_in, kv_in, lists_in, counts_in, q, kv, transit, lists, counts,
+                  sz, st, sq_sem, rz, rt, rq, s_mate, s_far, s_y, s_relay, s_cross, arrive, sl, rl):
     hd, sq, z, c, y, x, b, k = place()
-    p = 2 * y + k
-    frame = 2 * p + c
+    frame = 4 * y + 2 * k + c
+    started = []
 
     def dev(h, s):
         return {"head": h, "seq": s}
 
-    def pair_dev(pt):
-        return dev(hd, 4 * (pt // 2) + 2 * b + pt % 2)
+    def send(pred, make):
+        @pl.when(pred)
+        def _():
+            make().start()
+        started.append((pred, make))
 
     sibling = dev(2 * z + 1 - c, sq)
-
-    def home(r, bb):
-        zt = (z + r) % 8
-        return zt, 2 * zt + x % 2, 4 * y + 2 * bb + x // 2
+    mate = dev(hd, 4 * y + 2 * b + 1 - k)
+    opposite = dev(hd, 4 * y + 3 - x)
+    row_up, row_down, row_two = (y + 1) % 4, (y + 3) % 4, (y + 2) % 4
+    up = dev(hd, 4 * row_up + x)
+    down = dev(hd, 4 * row_down + x)
 
     barrier = pltpu.get_barrier_semaphore()
+    for t in range(1, HEADS):
+        pl.semaphore_signal(barrier, 1, device_id=dev((hd + t) % HEADS, sq), device_id_type=MESH)
+    for device in (mate, opposite, up, down):
+        pl.semaphore_signal(barrier, 1, device_id=device, device_id_type=MESH)
     for t in range(HEADS):
         @pl.when((t != hd) | (frame != sq))
         def _():
             pl.semaphore_signal(barrier, 1, device_id=dev(t, frame), device_id_type=MESH)
-    for d in range(1, PAIRS):
-        pl.semaphore_signal(barrier, 1, device_id=pair_dev((p + d) % PAIRS), device_id_type=MESH)
-    pl.semaphore_signal(barrier, 1, device_id=sibling, device_id_type=MESH)
     self_home = (frame == sq).astype(jnp.int32)
-    pl.semaphore_wait(barrier, HEADS - self_home + PAIRS)
-
-    def phase1(src, dst, send, recv, r, bb, act):
-        zt, ht, st = home(r, bb)
-        head = 2 * zt + bb
-        remote = (ht != hd) | (st != sq)
-
-        @pl.when(remote)
-        def _():
-            cp = pltpu.make_async_remote_copy(src.at[head], dst, send.at[r * 2 + bb], recv.at[hd],
-                                              device_id=dev(ht, st), device_id_type=MESH)
-            cp.start() if act else cp.wait_send()
-
-        if act:
-            @pl.when(jnp.logical_not(remote))
-            def _():
-                pltpu.make_async_copy(src.at[head], dst, recv.at[hd]).start()
-
-    kv_home = kv.at[sq * PER + hd]
-    q_home = q.at[hd]
-    for r in range(8):
+    pl.semaphore_wait(barrier, HEADS - 1 + 4 + HEADS - self_home)
+
+    def line(src, dst, send_sem, recv_sem, target, seq):
+        remote = (target != hd) | (seq != sq)
+        send(remote, lambda: pltpu.make_async_remote_copy(src, dst, send_sem, recv_sem,
+                                                          device_id=dev(target, seq), device_id_type=MESH))
+
+        @pl.when(jnp.logical_not(remote))
+        def _():
+            pltpu.make_async_copy(src, dst, recv_sem).start()
+
+    for r, hop in enumerate(HOPS):
+        zt = (z + hop + 8) % 8
+        line(kv_in.at[2 * zt + b], kv.at[sq * PER + hd], sz.at[r], rz.at[hd], 2 * zt + k, sq)
+        line(kv_in.at[2 * zt + 1 - b], transit.at[hd], st.at[r], rt.at[hd], 2 * zt + k, sq)
+    for r, hop in enumerate(HOPS):
+        zt = (z + hop + 8) % 8
         for bb in range(2):
-            phase1(kv_in, kv_home, s1kv, r1kv, r, bb, True)
-    for r in range(8):
-        for bb in range(2):
-            phase1(q_in, q_home, s1q, r1q, r, bb, True)
-
-    def list_copies(rows, device):
-        return (pltpu.make_async_remote_copy(lists_in.at[pl.ds(rows * PER, PER)], lists, sl.at[0], rl.at[0],
-                                             device_id=device, device_id_type=MESH),
-                pltpu.make_async_remote_copy(counts_in, counts, sl.at[1], rl.at[1],
-                                             device_id=device, device_id_type=MESH))
-
-    @pl.when(b == c)
+            line(q_in.at[2 * zt + bb], q.at[hd], sq_sem.at[2 * r + bb], rq.at[hd], 2 * zt + k, 4 * y + 2 * bb + b)
+
+    mine = b == c
+    other_rows = lists_in.at[pl.ds((4 * y + 2 * k + 1 - c) * PER, PER)]
+    my_rows = lists_in.at[pl.ds(frame * PER, PER)]
+    send(mine, lambda: pltpu.make_async_remote_copy(other_rows, lists, sl.at[0], rl.at[0],
+                                                    device_id=sibling, device_id_type=MESH))
+    send(mine, lambda: pltpu.make_async_remote_copy(counts_in, counts, sl.at[1], rl.at[1],
+                                                    device_id=sibling, device_id_type=MESH))
+
+    @pl.when(mine)
     def _():
-        for cp in list_copies(4 * y + 2 * k + 1 - c, sibling):
-            cp.start()
-        pltpu.make_async_copy(lists_in.at[pl.ds(frame * PER, PER)], lists, rl.at[0]).start()
+        pltpu.make_async_copy(my_rows, lists, rl.at[0]).start()
         pltpu.make_async_copy(counts_in, counts, rl.at[1]).start()
 
     def span(fr, m):
         return kv.at[pl.ds(fr * PER + m * CH, CH)]
 
-    def lane_copy(d, m):
-        part = span(frame, m)
-        return pltpu.make_async_remote_copy(part, part, s2.at[d + PAIRS - 1, m], r2.at[p, m],
-                                            device_id=pair_dev(p + d), device_id_type=MESH)
-
-    def lane_arrival(pt, m):
-        part = span(2 * pt + c, m)
-        return pltpu.make_async_remote_copy(part, part, s2.at[0, 0], r2.at[pt, m],
-                                            device_id=sibling, device_id_type=MESH)
-
-    def cross_copy(pt, m, core):
-        part = span(2 * pt + core, m)
-        return pltpu.make_async_remote_copy(part, part, s3.at[pt, m], r3.at[pt, m],
-                                            device_id=sibling, device_id_type=MESH)
-
-    def inside(pt):
-        return (pt >= 0) & (pt < PAIRS)
-
-    def crosses(dp, m, core):
-        if abs(dp) <= 1:
-            return True
-        if dp == 2:
-            return (core == 0) | (m == 0)
-        if dp == -2:
-            return (core == 1) | (m == 0)
-        return m == 0
-
-    def own(m):
-        for t in range(CH):
-            j = m * CH + t
-            pltpu.make_async_copy(kv.at[frame * PER + j], kv.at[frame * PER + j], r1kv.at[j]).wait()
-        for d in (1, -1, 2, -2):
-            @pl.when(inside(p + d))
-            def _():
-                lane_copy(d, m).start()
-        cross_copy(p, m, c).start()
-        for d in range(3, PAIRS):
-            for sgn in (1, -1):
-                @pl.when(inside(p + sgn * d) & (m == 0))
-                def _():
-                    lane_copy(sgn * d, m).start()
-
-    def relay(m):
-        for d in (1, -1, 2, -2):
-            pt = p + d
-
-            @pl.when(inside(pt))
-            def _():
-                lane_arrival(pt, m).wait_recv()
-
-            @pl.when(inside(pt) & crosses(d, m, c))
-            def _():
-                cross_copy(pt, m, c).start()
-        for d in range(3, PAIRS):
-            for sgn in (1, -1):
-                pt = p + sgn * d
-
-                @pl.when(inside(pt) & (m == 0))
-                def _():
-                    lane_arrival(pt, m).wait_recv()
-                    cross_copy(pt, m, c).start()
-
-    order = [(z // 2 + 4 - i) % 4 for i in range(4)]
-    own(order[0])
-    own(order[1])
-    relay(order[0])
-    own(order[2])
-    relay(order[1])
-    own(order[3])
-    relay(order[2])
-    relay(order[3])
+    def chunk(src, fr, m, sem, device):
+        return pltpu.make_async_remote_copy(src, span(fr, m), sem, arrive.at[fr, m],
+                                            device_id=device, device_id_type=MESH)
+
+    def arrived(pred, fr, m):
+        @pl.when(pred)
+        def _():
+            pltpu.make_async_copy(span(fr, m), span(fr, m), arrive.at[fr, m]).wait()
+
+    def cross(pred, fr, m):
+        send(pred, lambda: chunk(span(fr, m), fr, m, s_cross.at[fr, m], sibling))
+
+    def down_received(first, m):
+        return (m == 0) | ((y > 0) & (k == 0)) if first else (m == 0) | (y > 0)
+
+    def up_received(first, m):
+        return (m == 0) | (y < 3) if first else (m == 0) | ((y < 3) & (k == 1))
+
+    def down_crosses(first, m, core):
+        if first:
+            return (m == 0) | ((y > 0) & (k == 0) & (core == 1))
+        return (m == 0) | ((y > 0) & ((k == 0) | (core == 1)))
+
+    def up_crosses(first, m, core):
+        if first:
+            return (m == 0) | ((y < 3) & ((k == 1) | (core == 0)))
+        return (m == 0) | ((y < 3) & (k == 1) & (core == 0))
+
+    own = 4 * y + 2 * b + c
+    guest = 4 * y + 2 * (1 - b) + c
+    lands = k == c
+    relays = k != c
+
+    def from_here(fr, first, slot, m):
+        send((m == 0) | ((y < 3) & ((k == 0) | jnp.logical_not(first))),
+             lambda: chunk(span(fr, m), fr, m, s_y.at[slot, 0, m], up))
+        send((m == 0) | ((y > 0) & ((k == 1) | first)),
+             lambda: chunk(span(fr, m), fr, m, s_y.at[slot, 1, m], down))
+        cross(True, fr, m)
+
+    def step_own(m):
+        @pl.when(lands)
+        def _():
+            for t in range(CH):
+                j = m * CH + t
+                pltpu.make_async_copy(kv.at[own * PER + j], kv.at[own * PER + j], rz.at[j]).wait()
+        arrived(relays, own, m)
+        send(lands, lambda: chunk(span(own, m), own, m, s_mate.at[m], mate))
+
+        @pl.when(lands)
+        def _():
+            for t in range(CH):
+                j = m * CH + t
+                pltpu.make_async_copy(transit.at[j], transit.at[j], rt.at[j]).wait()
+        send(lands, lambda: chunk(transit.at[pl.ds(m * CH, CH)], own, m, s_far.at[m], opposite))
+        from_here(own, b == 0, 0, m)
+
+    def step_guest(m):
+        arrived(True, guest, m)
+        send(relays, lambda: chunk(span(guest, m), guest, m, s_mate.at[m], mate))
+        from_here(guest, b == 1, 1, m)
+
+    def step_rows(m):
+        for first in (True, False):
+            fr = 4 * row_down + c + (0 if first else 2)
+            arrived(down_received(first, m), fr, m)
+            cross(down_crosses(first, m, c), fr, m)
+            if first:
+                send(m == 0, lambda: chunk(span(fr, m), fr, m, s_relay.at[0], up))
+            fu = 4 * row_up + c + (0 if first else 2)
+            arrived(up_received(first, m), fu, m)
+            cross(up_crosses(first, m, c), fu, m)
+            if not first:
+                send(m == 0, lambda: chunk(span(fu, m), fu, m, s_relay.at[1], down))
+
+    a, odd = z // 2, z % 2
+    order = [a, (a + 3 + 2 * odd) % 4, (a + 1 + 2 * odd) % 4, (a + 2) % 4]
+    step_own(order[0])
+    step_own(order[1])
+    step_guest(order[0])
+    step_own(order[2])
+    step_guest(order[1])
+    step_rows(order[0])
+    step_own(order[3])
+    step_guest(order[2])
+    step_rows(order[1])
+    step_guest(order[3])
+    step_rows(order[2])
+    step_rows(order[3])
+    for second in range(2):
+        fr = 4 * row_two + c + 2 * second
+        arrived(True, fr, 0)
+        cross(True, fr, 0)
 
     for j in range(PER):
-        pltpu.make_async_copy(q.at[j], q.at[j], r1q.at[j]).wait()
-    pltpu.make_async_copy(lists_in.at[pl.ds(frame * PER, PER)], lists, rl.at[0]).wait()
+        pltpu.make_async_copy(q.at[j], q.at[j], rq.at[j]).wait()
+    pltpu.make_async_copy(my_rows, lists, rl.at[0]).wait()
     pltpu.make_async_copy(counts_in, counts, rl.at[1]).wait()
-
-    @pl.when(b == c)
-    def _():
-        for cp in list_copies(4 * y + 2 * k + 1 - c, sibling):
-            cp.wait_send()
-
     for m in range(4):
-        for d in range(1 - PAIRS, PAIRS):
-            if d != 0 and (abs(d) <= 2 or m == 0):
-                @pl.when(inside(p + d))
-                def _():
-                    lane_copy(d, m).wait_send()
-            if abs(d) <= 2 or m == 0:
-                @pl.when(inside(p + d) & crosses(d, m, c))
-                def _():
-                    cross_copy(p + d, m, c).wait_send()
-
-                @pl.when(inside(p + d) & crosses(d, m, 1 - c))
-                def _():
-                    cross_copy(p + d, m, 1 - c).wait_recv()
-    for r in range(8):
-        for bb in range(2):
-            phase1(kv_in, kv_home, s1kv, r1kv, r, bb, False)
-            phase1(q_in, q_home, s1q, r1q, r, bb, False)
+        for first in (True, False):
+            lane = 1 - c + (0 if first else 2)
+            arrived(True, 4 * y + lane, m)
+            arrived(down_crosses(first, m, 1 - c), 4 * row_down + lane, m)
+            arrived(up_crosses(first, m, 1 - c), 4 * row_up + lane, m)
+            if m == 0:
+                arrived(True, 4 * row_two + lane, m)
+    for pred, make in started:
+        @pl.when(pred)
+        def _():
+            make().wait_send()
 
 
 def attend_kernel(lists, counts, q_ref, kv_hbm, o_ref, kv, s0, s1, acc, den, sems):
@@ -393,15 +400,15 @@
         in_specs=[vmem] * 5,
         out_specs=(vmem, vmem),
         name="prepare",
-    )(projected.reshape(TILE, 3 * HEADS * HD), cosine, sine, query_gain[None], key_gain[None])
-    q, kv, lists, counts = pl.pallas_call(
+    )(jnp.transpose(projected, (1, 0, 2)), cosine, sine, query_gain[None], key_gain[None])
+    q, kv, _, lists, counts = pl.pallas_call(
         spread_kernel,
-        out_shape=(sds((PER, TILE, HD), bf16), sds((FRAMES * PER, 2, TILE, HD), bf16),
+        out_shape=(sds((PER, TILE, HD), bf16), sds((FRAMES * PER, 2, TILE, HD), bf16), sds((PER, 2, TILE, HD), bf16),
                    sds((PER, 96), jnp.int32), sds((1, FRAMES * PER), jnp.int32)),
         in_specs=[hbm] * 4,
-        out_specs=(hbm,) * 4,
-        scratch_shapes=[dma((16,)), dma((16,)), dma((16,)), dma((16,)), dma((2 * PAIRS - 1, 4)), dma((PAIRS, 4)),
-                        dma((PAIRS, 4)), dma((PAIRS, 4)), dma((2,)), dma((2,))],
+        out_specs=(hbm,) * 5,
+        scratch_shapes=[dma((8,)), dma((8,)), dma((16,)), dma((16,)), dma((16,)), dma((16,)), dma((4,)), dma((4,)),
+                        dma((2, 2, 4)), dma((2,)), dma((FRAMES, 4)), dma((FRAMES, 4)), dma((2,)), dma((2,))],
         compiler_params=pltpu.CompilerParams(collective_id=0, has_side_effects=True),
         name="spread",
     )(q_own, kv_own, tile_lists[0], tile_counts)

time: 190 us -> 165 us (0.87)
  Pallas kernels: 178 us -> 156 us
  local copies, waits for them, and re-layouts: 10.9 us -> 8.28 us
    pallas_call x1, Pallas kernels: 110 us -> 76.2 us  [local(): pl.pallas_call(spread_kernel, out_shape=(sds((PER, TILE, HD), bf16), sds(...]
    pallas_call x1, Pallas kernels: 17.4 us -> 29.2 us  [local(): pl.pallas_call(return_kernel, out_shape=sds((TILE, HEADS * HD), bf16), in...]
    unnamed x13 -> x10, local copies, waits for them, and re-layouts: 7.7 us -> 6.71 us
where the time goes in v2:
time: 165 us
  Pallas kernels  156 us (95%)
  local copies, waits for them, and re-layouts  8.28 us (5%)
    pallas_call x1, Pallas kernels, local(): pl.pallas_call(spread_kernel, out_shape=(sds((PER, TILE, HD), bf16), sds(...  76.2 us
    pallas_call x1, Pallas kernels, local(): pl.pallas_call(attend_kernel, out_shape=sds((PER, TILE, HD), bf16), in_sp...  42.6 us
    pallas_call x1, Pallas kernels, local(): pl.pallas_call(return_kernel, out_shape=sds((TILE, HEADS * HD), bf16), in...  29.2 us
    pallas_call x1, Pallas kernels, local(): pl.pallas_call(prepare_kernel, out_shape=(sds((HEADS, TILE, HD), bf16), s...  7.98 us
    unnamed x10, local copies, waits for them, and re-layouts  6.71 us

profile of v2, /device:TPU:17, one launch (start us, length us, event | category | flops | bytes accessed | tf_op | source)
XLA Modules:
  0.0 165.0 jit_solution(4993695610229104050)
XLA Ops:
  0.0 0.1 fusion.6
  0.1 0.1 fusion.4
  0.2 1.6 copy.9
  1.8 0.5 multiply_sine_fusion
  2.4 0.8 concatenate.6.cos
  3.2 0.8 concatenate.7.sin
  3.9 8.0 %prepare.1 = (bf16[16,128,128]{2,1,0:T(8,128)(2,1)}, bf16[16,2,128,128]{3,2,1,0:T(8,128)(2,1)}) custom-call(bf16[3,128,2048]{2,1,0:T(8,128)(2,1)} %bitcast.4, f32[128,128]{1,0:T(8,128)} %concatenate.6.cos, f32[128,128]{1,0:T(8,128)} %concatenate.7.sin, f32[1,128]{1,0:T(1,128)} %bitcast.6, f32[1,128]{1,0:T(1,128)} %bitcast.7), custom_call_target="tpu_custom_call" | custom-call | tf_op jit(solution)/shard_map/prepare/pallas_call | solution.py:397
  11.9 76.2 %spread.1 = (bf16[16,128,128]{2,1,0:T(8,128)(2,1)}, bf16[256,2,128,128]{3,2,1,0:T(8,128)(2,1)}, bf16[16,2,128,128]{3,2,1,0:T(8,128)(2,1)}, s32[16,96]{1,0:T(8,128)}, s32[1,256]{1,0:T(1,128)}) custom-call(bf16[16,128,128]{2,1,0:T(8,128)(2,1)} %get-tuple-element.11.q_in, bf16[16,2,128,128]{3,2,1,0:T(8,128)(2,1)} %get-tuple-element.12.kv_in, ...), custom_call_target="tpu_custom_call" | custom-call | tf_op jit(solution)/shard_map/spread/pallas_call | solution.py:404
  88.2 0.0 copy-start.1
  88.2 1.0 copy-done.1
  89.2 0.0 copy-start.2
  89.2 0.7 copy-done.2
  89.9 0.0 copy-start.3
  89.9 0.7 copy-done.3
  90.6 42.6 %attend.1.o_in = bf16[16,128,128]{2,1,0:T(8,128)(2,1)S(1)} custom-call(s32[16,96]{1,0:T(8,128)S(1)} %copy-done.2, s32[1,256]{1,0:T(1,128)S(1)} %copy-done.3, bf16[16,128,128]{2,1,0:T(8,128)(2,1)S(1)} %copy-done.1, bf16[256,2,128,128]{3,2,1,0:T(8,128)(2,1)} %get-tuple-element.16.kv_hbm), custom_call_target="tpu_custom_call" | custom-call | tf_op jit(solution)/shard_map/attend/pallas_call | solution.py:415
  133.1 0.0 copy-start
  133.1 0.8 copy-done
  133.9 29.2 %give_back.1 = bf16[128,2048]{1,0:T(8,128)(2,1)} custom-call(bf16[16,128,128]{2,1,0:T(8,128)(2,1)} %copy-done), custom_call_target="tpu_custom_call" | custom-call | tf_op jit(solution)/shard_map/give_back/pallas_call | solution.py:426
  163.2 1.9 %copy.11 = bf16[128,2048]{1,0:T(8,128)(2,1)} copy(bf16[128,2048]{1,0:T(8,128)(2,1)} %give_back.1) | data formatting | bytes 1048576
  (5 shorter events, 0.0 us)
Async XLA Ops:
  88.2 1.0 copy-start.1
  89.2 0.7 copy-start.2
  89.9 0.7 copy-start.3
  133.1 0.8 copy-start

commit v3 on v2

--- a/solution.py
+++ b/solution.py
@@ -16,11 +16,11 @@
 FRAMES = 16
 PER = 16
 CH = 4
+MAXK = 96
 THETA = 256.0
 SCALE = math.log2(math.e) / math.sqrt(HD)
-G = 8
-SUB = 2
-HOPS = (0, 1, -1, 2, -2, 3, -3, 4)
+G = 16
+NONE = FRAMES * PER
 MESH = pl.DeviceIdType.MESH
 f32 = jnp.float32
 bf16 = jnp.bfloat16
@@ -55,23 +55,6 @@
     return jnp.where(lane < first, near, far)
 
 
-def prepare_kernel(proj, cos, sin, qg, kg, q_out, kv_out):
-    cosine = cos[...]
-    sine = sin[...]
-    for h in range(HEADS):
-        for part, gain in ((0, qg), (1, kg)):
-            lo = h * HD
-            field = proj[part, :, lo:lo + HD].astype(f32)
-            mean = jnp.sum(field * field, axis=1, keepdims=True) * (1.0 / HD)
-            field = field * lax.rsqrt(mean + 1e-06) * gain[...]
-            turned = (field * cosine + partner(field) * sine).astype(bf16)
-            if part == 0:
-                q_out[h] = turned
-            else:
-                kv_out[h, 0] = turned
-        kv_out[h, 1] = proj[2, :, h * HD:(h + 1) * HD]
-
-
 def place():
     hd = lax.axis_index("head")
     sq = lax.axis_index("seq")
@@ -81,8 +64,8 @@
     return hd, sq, z, c, y, x, b, k
 
 
-def spread_kernel(q_in, kv_in, lists_in, counts_in, q, kv, transit, lists, counts,
-                  sz, st, sq_sem, rz, rt, rq, s_mate, s_far, s_y, s_relay, s_cross, arrive, sl, rl):
+def spread_kernel(proj, cos, sin, qg, kg, lists_in, counts_in, q, kv, transit, lists, counts,
+                  kv_in, q_in, sz, st, sq_sem, rz, rt, rq, s_mate, s_far, s_y, s_relay, s_cross, arrive, sl, rl):
     hd, sq, z, c, y, x, b, k = place()
     frame = 4 * y + 2 * k + c
     started = []
@@ -115,23 +98,58 @@
     self_home = (frame == sq).astype(jnp.int32)
     pl.semaphore_wait(barrier, HEADS - 1 + 4 + HEADS - self_home)
 
-    def line(src, dst, send_sem, recv_sem, target, seq):
+    def line(src, dst, send_sem, recv_sem, target, seq, act):
         remote = (target != hd) | (seq != sq)
-        send(remote, lambda: pltpu.make_async_remote_copy(src, dst, send_sem, recv_sem,
-                                                          device_id=dev(target, seq), device_id_type=MESH))
-
-        @pl.when(jnp.logical_not(remote))
-        def _():
-            pltpu.make_async_copy(src, dst, recv_sem).start()
-
-    for r, hop in enumerate(HOPS):
-        zt = (z + hop + 8) % 8
-        line(kv_in.at[2 * zt + b], kv.at[sq * PER + hd], sz.at[r], rz.at[hd], 2 * zt + k, sq)
-        line(kv_in.at[2 * zt + 1 - b], transit.at[hd], st.at[r], rt.at[hd], 2 * zt + k, sq)
-    for r, hop in enumerate(HOPS):
-        zt = (z + hop + 8) % 8
+
+        @pl.when(remote)
+        def _():
+            cp = pltpu.make_async_remote_copy(src, dst, send_sem, recv_sem,
+                                              device_id=dev(target, seq), device_id_type=MESH)
+            cp.start() if act else cp.wait_send()
+
+        if act:
+            @pl.when(jnp.logical_not(remote))
+            def _():
+                pltpu.make_async_copy(src, dst, recv_sem).start()
+
+    def peer(r):
+        far = (r + 1) // 2
+        return (z + jnp.where(r % 2 == 1, far, 8 - far)) % 8
+
+    def lanes(h):
+        return pl.ds(pl.multiple_of(h * HD, HD), HD)
+
+    def normed(part, gain, h):
+        field = proj[part, :, lanes(h)].astype(f32)
+        mean = jnp.sum(field * field, axis=1, keepdims=True) * (1.0 / HD)
+        field = field * lax.rsqrt(mean + 1e-06) * gain[...]
+        return (field * cos[...] + partner(field) * sin[...]).astype(bf16)
+
+    def line_kv(r, act):
+        zt = peer(r)
+        for h, dst, send_sem, recv_sem in ((2 * zt + b, kv.at[sq * PER + hd], sz, rz),
+                                           (2 * zt + 1 - b, transit.at[hd], st, rt)):
+            if act:
+                kv_in[h, 0] = normed(1, kg, h)
+                kv_in[h, 1] = jnp.transpose(proj[2, :, lanes(h)])
+            line(kv_in.at[h], dst, send_sem.at[r], recv_sem.at[hd], 2 * zt + k, sq, act)
+
+    def line_q(r, act):
+        zt = peer(r)
         for bb in range(2):
-            line(q_in.at[2 * zt + bb], q.at[hd], sq_sem.at[2 * r + bb], rq.at[hd], 2 * zt + k, 4 * y + 2 * bb + b)
+            h = 2 * zt + bb
+            if act:
+                q_in[h] = normed(0, qg, h)
+            line(q_in.at[h], q.at[hd], sq_sem.at[2 * r + bb], rq.at[hd], 2 * zt + k, 4 * y + 2 * bb + b, act)
+
+    def each(step, act):
+        def body(r, _):
+            step(r, act)
+            return 0
+        lax.fori_loop(0, 8, body, 0)
+
+    each(line_kv, True)
+    each(line_q, True)
 
     mine = b == c
     other_rows = lists_in.at[pl.ds((4 * y + 2 * k + 1 - c) * PER, PER)]
@@ -259,11 +277,16 @@
         @pl.when(pred)
         def _():
             make().wait_send()
-
-
-def attend_kernel(lists, counts, q_ref, kv_hbm, o_ref, kv, s0, s1, acc, den, sems):
+    each(line_kv, False)
+    each(line_q, False)
+
+
+def attend_kernel(lists_hbm, counts_hbm, q_hbm, kv_hbm, o_ref, kv, q_ref, lists, counts, s0, s1, acc, ids, owner, sems):
     _, _, _, c, y, _, _, k = place()
     frame = 4 * y + 2 * k + c
+
+    small = [pltpu.make_async_copy(src, dst, sems.at[FRAMES + n])
+             for n, (src, dst) in enumerate(((lists_hbm, lists), (counts_hbm, counts), (q_hbm, q_ref)))]
 
     def loads(act):
         for fr in range(FRAMES):
@@ -279,65 +302,75 @@
                 part = pl.ds(fr * PER, CH)
                 act(pltpu.make_async_copy(kv_hbm.at[part], kv.at[part], sems.at[fr]))
 
+    for cp in small:
+        cp.start()
     loads(lambda cp: cp.start())
     acc[...] = jnp.zeros_like(acc)
-    den[...] = jnp.zeros_like(den)
-
-    def count(i):
-        return counts[0, frame * PER + i]
-
-    total = lax.fori_loop(0, PER, lambda i, t: t + (count(i) + G - 1) // G, 0)
+    kv[NONE] = jnp.zeros((2, TILE, HD), bf16)
+    for cp in small:
+        cp.wait()
+
+    def plan(i, e):
+        n = counts[0, frame * PER + i]
+
+        def chunk(g, e):
+            owner[e] = i
+            for u in range(G):
+                j = g * G + u
+                ids[e * G + u] = jnp.where(j < n, lists[i, j], NONE)
+            return e + 1
+
+        return lax.fori_loop(0, (n + G - 1) // G, chunk, e)
+
+    total = lax.fori_loop(0, PER, plan, jnp.int32(0))
+    owner[total] = 0
+    for u in range(G):
+        ids[total * G + u] = NONE
+    half = (total + 1) // 2
     loads(lambda cp: cp.wait())
 
-    def following(i, g):
-        stay = ((g + 1) * G < count(i)) | (i == PER - 1)
-        return jnp.where(stay, i, i + 1), jnp.where(stay, g + 1, 0)
-
-    def ids(i, g):
-        last = count(i) - 1
-        return [lists[i, jnp.minimum(g * G + u, last)] for u in range(G)]
-
-    def score(i, g, s):
-        chosen = ids(i, g)
-        q = q_ref[i]
-        for w in range(0, G, SUB):
-            keys = jnp.concatenate([kv[t, 0] for t in chosen[w:w + SUB]], 0)
-            s[:, w * TILE:(w + SUB) * TILE] = lax.dot_general(
-                q, keys, (((1,), (1,)), ((), ())), preferred_element_type=f32)
-
-    def weigh(i, g, s):
-        chosen = ids(i, g)
-        n = count(i)
-        d = jnp.zeros((TILE, TILE), f32)
-        a = jnp.zeros((TILE, HD), f32)
-        for w in range(0, G, SUB):
-            e = jnp.exp2(s[:, w * TILE:(w + SUB) * TILE] * SCALE)
-            parts = [jnp.where(g * G + w + u < n, e[:, u * TILE:(u + 1) * TILE], 0.0) for u in range(SUB)]
-            for part in parts:
-                d = d + part
-            weights = jnp.concatenate(parts, 1).astype(bf16)
-            values = jnp.concatenate([kv[t, 1] for t in chosen[w:w + SUB]], 0)
-            a = a + lax.dot_general(weights, values, (((1,), (0,)), ((), ())), preferred_element_type=f32)
-        acc[i] += a
-        den[i] += d
-
-    zero = jnp.int32(0)
-    score(zero, zero, s0)
-
-    def body(_, state):
-        i, g = state
-        i1, g1 = following(i, g)
-        score(i1, g1, s1)
-        weigh(i, g, s0)
-        i2, g2 = following(i1, g1)
-        score(i2, g2, s0)
-        weigh(i1, g1, s1)
-        return i2, g2
-
-    lax.fori_loop(0, (total + 1) // 2, body, (zero, zero))
+    def pair(e):
+        return jnp.where(e < half, e, total), jnp.where(half + e < total, half + e, total)
+
+    blank = jnp.zeros((TILE, HD), bf16)
+    ones = jnp.ones((16, TILE), bf16)
+    none = jnp.zeros((16, TILE), bf16)
+
+    def score(e, s):
+        left, right = pair(e)
+        queries = jnp.concatenate([jnp.concatenate([q_ref[owner[left]], blank], 1),
+                                   jnp.concatenate([blank, q_ref[owner[right]]], 1)], 0)
+        keys = jnp.concatenate([jnp.concatenate([kv[ids[left * G + u], 0], kv[ids[right * G + u], 0]], 1)
+                                for u in range(G)], 0)
+        s[...] = lax.dot_general(keys, queries, (((1,), (1,)), ((), ())), preferred_element_type=f32)
+
+    def weigh(e, s):
+        for side, chunk in enumerate(pair(e)):
+            weights, values, live = [], [], []
+            for u in range(G):
+                t = ids[chunk * G + u]
+                part = s[u * TILE:(u + 1) * TILE, side * TILE:(side + 1) * TILE]
+                weights.append(jnp.exp2(part * SCALE).astype(bf16))
+                values.append(kv[t, 1])
+                live.append(jnp.where(t < NONE, ones, none))
+            rows = jnp.concatenate([jnp.concatenate(values, 1), jnp.concatenate(live, 1)], 0)
+            acc[owner[chunk]] += lax.dot_general(rows, jnp.concatenate(weights, 0), (((1,), (0,)), ((), ())),
+                                                 preferred_element_type=f32)
+
+    score(jnp.int32(0), s0)
+
+    def body(h, _):
+        e = 2 * h
+        score(e + 1, s1)
+        weigh(e, s0)
+        score(e + 2, s0)
+        weigh(e + 1, s1)
+        return 0
+
+    lax.fori_loop(0, (half + 1) // 2, body, 0)
 
     def finish(i, _):
-        o_ref[i] = (acc[i] / jnp.sum(den[i], axis=1, keepdims=True)).astype(bf16)
+        o_ref[i] = jnp.transpose(acc[i, :HD] / acc[i, HD:HD + 1]).astype(bf16)
         return 0
 
     lax.fori_loop(0, PER, finish, 0)
@@ -389,44 +422,40 @@
     hd = lax.axis_index("head")
     sq = lax.axis_index("seq")
     vmem = pl.BlockSpec(memory_space=pltpu.VMEM)
-    smem = pl.BlockSpec(memory_space=pltpu.SMEM)
-    hbm = pl.BlockSpec(memory_space=pl.ANY)
+    hbm = pl.BlockSpec(memory_space=pltpu.HBM)
     sds = jax.ShapeDtypeStruct
     dma = pltpu.SemaphoreType.DMA
     cosine, sine = rope_tables(sq, hd)
-    q_own, kv_own = pl.pallas_call(
-        prepare_kernel,
-        out_shape=(sds((HEADS, TILE, HD), bf16), sds((HEADS, 2, TILE, HD), bf16)),
-        in_specs=[vmem] * 5,
-        out_specs=(vmem, vmem),
-        name="prepare",
-    )(jnp.transpose(projected, (1, 0, 2)), cosine, sine, query_gain[None], key_gain[None])
     q, kv, _, lists, counts = pl.pallas_call(
         spread_kernel,
         out_shape=(sds((PER, TILE, HD), bf16), sds((FRAMES * PER, 2, TILE, HD), bf16), sds((PER, 2, TILE, HD), bf16),
-                   sds((PER, 96), jnp.int32), sds((1, FRAMES * PER), jnp.int32)),
-        in_specs=[hbm] * 4,
+                   sds((PER, MAXK), jnp.int32), sds((1, FRAMES * PER), jnp.int32)),
+        in_specs=[vmem] * 5 + [hbm] * 2,
         out_specs=(hbm,) * 5,
-        scratch_shapes=[dma((8,)), dma((8,)), dma((16,)), dma((16,)), dma((16,)), dma((16,)), dma((4,)), dma((4,)),
+        scratch_shapes=[pltpu.VMEM((HEADS, 2, TILE, HD), bf16), pltpu.VMEM((HEADS, TILE, HD), bf16),
+                        dma((8,)), dma((8,)), dma((16,)), dma((16,)), dma((16,)), dma((16,)), dma((4,)), dma((4,)),
                         dma((2, 2, 4)), dma((2,)), dma((FRAMES, 4)), dma((FRAMES, 4)), dma((2,)), dma((2,))],
         compiler_params=pltpu.CompilerParams(collective_id=0, has_side_effects=True),
         name="spread",
-    )(q_own, kv_own, tile_lists[0], tile_counts)
+    )(jnp.transpose(projected, (1, 0, 2)), cosine, sine, query_gain[None], key_gain[None], tile_lists[0], tile_counts)
+    chunks = PER * (MAXK // G) + 1
     attended = pl.pallas_call(
         attend_kernel,
         out_shape=sds((PER, TILE, HD), bf16),
-        in_specs=[smem, smem, vmem, hbm],
+        in_specs=[hbm] * 4,
         out_specs=vmem,
-        scratch_shapes=[pltpu.VMEM((FRAMES * PER, 2, TILE, HD), bf16), pltpu.VMEM((TILE, G * TILE), f32),
-                        pltpu.VMEM((TILE, G * TILE), f32), pltpu.VMEM((PER, TILE, TILE), f32),
-                        pltpu.VMEM((PER, TILE, HD), f32), dma((FRAMES,))],
+        scratch_shapes=[pltpu.VMEM((FRAMES * PER + 1, 2, TILE, HD), bf16), pltpu.VMEM((PER, TILE, HD), bf16),
+                        pltpu.SMEM((PER, MAXK), jnp.int32), pltpu.SMEM((1, FRAMES * PER), jnp.int32),
+                        pltpu.VMEM((G * TILE, 2 * TILE), f32), pltpu.VMEM((G * TILE, 2 * TILE), f32),
+                        pltpu.VMEM((PER, HD + 16, TILE), f32), pltpu.SMEM((chunks * G,), jnp.int32),
+                        pltpu.SMEM((chunks,), jnp.int32), dma((FRAMES + 3,))],
         compiler_params=pltpu.CompilerParams(vmem_limit_bytes=40 * 1024 * 1024),
         name="attend",
     )(lists, counts, q, kv)
     return pl.pallas_call(
         return_kernel,
         out_shape=sds((TILE, HEADS * HD), bf16),
-        in_specs=[hbm],
+        in_specs=[vmem],
         out_specs=hbm,
         scratch_shapes=[dma((HEADS,)), dma((HEADS,))],
         compiler_params=pltpu.CompilerParams(collective_id=1, has_side_effects=True),

time: 165 us -> 153 us (0.927)
  the two profiles are of different devices: /device:TPU:17 before, /device:TPU:1 now
where the time goes in v3:
time: 153 us
  Pallas kernels  144 us (94%)
  local copies, waits for them, and re-layouts  8.28 us (5%)
    pallas_call x1, Pallas kernels, local(): pl.pallas_call(spread_kernel, out_shape=(sds((PER, TILE, HD), bf16), sds(...  72.8 us
    pallas_call x1, Pallas kernels, local(): pl.pallas_call(return_kernel, out_shape=sds((TILE, HEADS * HD), bf16), in...  42.6 us
    pallas_call x1, Pallas kernels, local(): pl.pallas_call(attend_kernel, out_shape=sds((PER, TILE, HD), bf16), in_sp...  28.2 us
    unnamed x10, local copies, waits for them, and re-layouts  6.73 us

profile of v3, /device:TPU:1, one launch (start us, length us, event | category | flops | bytes accessed | tf_op | source)
XLA Modules:
  0.0 152.7 jit_solution(1648607574566347497)
XLA Ops:
  0.0 0.1 fusion.6
  0.1 0.1 fusion.4
  0.2 1.6 %copy.9 = s32[1,256,96]{2,1,0:T(8,128)} copy(s32[1,256,96]{1,2,0:T(8,128)} %param.8) | data formatting | bytes 196608 | tf_op args[3]
  1.8 0.5 multiply_sine_fusion
  2.4 0.8 concatenate.6.cos
  3.1 0.8 concatenate.7.sin
  3.9 72.8 %spread.1 = (bf16[16,128,128]{2,1,0:T(8,128)(2,1)}, bf16[256,2,128,128]{3,2,1,0:T(8,128)(2,1)}, bf16[16,2,128,128]{3,2,1,0:T(8,128)(2,1)}, s32[16,96]{1,0:T(8,128)}, s32[1,256]{1,0:T(1,128)}) custom-call(bf16[3,128,2048]{2,1,0:T(8,128)(2,1)} %bitcast.4, f32[128,128]{1,0:T(8,128)} %concatenate.6.cos, f32[128,128]{1,0:T(8,128)} %concatenate.7.sin, ...), custom_call_target="tpu_custom_call" | custom-call | tf_op jit(solution)/shard_map/spread/pallas_call | solution.py:429
  76.7 0.0 copy-start.1
  76.7 1.0 copy-done.1
  77.8 0.0 copy-start.2
  77.8 0.7 copy-done.2
  78.5 0.0 copy-start.3
  78.5 0.7 copy-done.3
  79.2 28.2 %attend.1.o_in = bf16[16,128,128]{2,1,0:T(8,128)(2,1)S(1)} custom-call(s32[16,96]{1,0:T(8,128)S(1)} %copy-done.2, s32[1,256]{1,0:T(1,128)S(1)} %copy-done.3, bf16[16,128,128]{2,1,0:T(8,128)(2,1)S(1)} %copy-done.1, bf16[256,2,128,128]{3,2,1,0:T(8,128)(2,1)} %get-tuple-element.12.kv_hbm), custom_call_target="tpu_custom_call" | custom-call | tf_op jit(solution)/shard_map/attend/pallas_call | solution.py:442
  107.4 0.0 copy-start
  107.4 0.8 copy-done
  108.2 42.6 %give_back.1 = bf16[128,2048]{1,0:T(8,128)(2,1)} custom-call(bf16[16,128,128]{2,1,0:T(8,128)(2,1)} %copy-done), custom_call_target="tpu_custom_call" | custom-call | tf_op jit(solution)/shard_map/give_back/pallas_call | solution.py:455
  150.8 1.9 %copy.11 = bf16[128,2048]{1,0:T(8,128)(2,1)} copy(bf16[128,2048]{1,0:T(8,128)(2,1)} %give_back.1) | data formatting | bytes 1048576
  (5 shorter events, 0.0 us)
Async XLA Ops:
  76.7 1.0 copy-start.1
  77.8 0.7 copy-start.2
  78.5 0.7 copy-start.3
  107.4 0.8 copy-start

commit v4 on v3

--- a/solution.py
+++ b/solution.py
@@ -3,6 +3,7 @@
 
 import jax
 import jax.numpy as jnp
+import numpy as np
 from jax import lax
 from jax.experimental import pallas as pl
 from jax.experimental.pallas import tpu as pltpu
@@ -21,27 +22,29 @@
 SCALE = math.log2(math.e) / math.sqrt(HD)
 G = 16
 NONE = FRAMES * PER
+
 MESH = pl.DeviceIdType.MESH
 f32 = jnp.float32
 bf16 = jnp.bfloat16
 
 
 def rope_tables(sq, hd):
-    tokens = hd * TILE + jnp.arange(TILE, dtype=jnp.int32)
-    row = tokens // GW
-    column = tokens % GW
-    frame = jnp.full((TILE,), sq, jnp.int32)
     first = HD // 8
     second = (HD - first) // 2
-    cosines, sines = [], []
-    for coordinate, extent in zip((frame, row, column), (first, second, HD - first - second)):
+    rates = np.zeros((3, 1, HD), np.float32)
+    sign = np.ones((1, HD), np.float32)
+    offset = 0
+    for axis, extent in enumerate((first, second, HD - first - second)):
         middle = extent // 2
-        inverse = THETA ** (-2.0 * jnp.arange(middle, dtype=f32) / extent)
-        angles = coordinate.astype(f32)[:, None] * inverse[None, :]
-        c, s = jnp.cos(angles), jnp.sin(angles)
-        cosines += [c, c]
-        sines += [-s, s]
-    return jnp.concatenate(cosines, 1), jnp.concatenate(sines, 1)
+        part = THETA ** (-2.0 * np.arange(middle) / extent)
+        rates[axis, 0, offset:offset + extent] = np.concatenate([part, part])
+        sign[0, offset:offset + middle] = -1.0
+        offset += extent
+    token = np.arange(TILE)[:, None]
+    row = (hd * (TILE // GW) + token // GW).astype(f32)
+    column = (token % GW).astype(np.float32)
+    angles = sq.astype(f32) * rates[0] + row * rates[1] + column * rates[2]
+    return jnp.cos(angles), jnp.sin(angles) * sign
 
 
 def partner(field):
@@ -152,16 +155,14 @@
     each(line_q, True)
 
     mine = b == c
-    other_rows = lists_in.at[pl.ds((4 * y + 2 * k + 1 - c) * PER, PER)]
-    my_rows = lists_in.at[pl.ds(frame * PER, PER)]
-    send(mine, lambda: pltpu.make_async_remote_copy(other_rows, lists, sl.at[0], rl.at[0],
+    send(mine, lambda: pltpu.make_async_remote_copy(lists_in, lists, sl.at[0], rl.at[0],
                                                     device_id=sibling, device_id_type=MESH))
     send(mine, lambda: pltpu.make_async_remote_copy(counts_in, counts, sl.at[1], rl.at[1],
                                                     device_id=sibling, device_id_type=MESH))
 
     @pl.when(mine)
     def _():
-        pltpu.make_async_copy(my_rows, lists, rl.at[0]).start()
+        pltpu.make_async_copy(lists_in, lists, rl.at[0]).start()
         pltpu.make_async_copy(counts_in, counts, rl.at[1]).start()
 
     def span(fr, m):
@@ -263,7 +264,7 @@
 
     for j in range(PER):
         pltpu.make_async_copy(q.at[j], q.at[j], rq.at[j]).wait()
-    pltpu.make_async_copy(my_rows, lists, rl.at[0]).wait()
+    pltpu.make_async_copy(lists_in, lists, rl.at[0]).wait()
     pltpu.make_async_copy(counts_in, counts, rl.at[1]).wait()
     for m in range(4):
         for first in (True, False):
@@ -281,12 +282,23 @@
     each(line_q, False)
 
 
-def attend_kernel(lists_hbm, counts_hbm, q_hbm, kv_hbm, o_ref, kv, q_ref, lists, counts, s0, s1, acc, ids, owner, sems):
-    _, _, _, c, y, _, _, k = place()
+def attend_kernel(lists_hbm, counts_hbm, q_hbm, kv_hbm, out, kv, q, lists, counts, s0, s1, acc, ids, done, sems,
+                  send, recv):
+    hd, sq, z, c, y, x, b, k = place()
     frame = 4 * y + 2 * k + c
+    head = 2 * z + b
+
+    barrier = pltpu.get_barrier_semaphore()
+    self_home = (frame == sq).astype(jnp.int32)
+    for h in range(HEADS):
+        hs, ss = 2 * (h // 2) + k, 4 * y + 2 * (h % 2) + b
+
+        @pl.when((hs != hd) | (ss != sq))
+        def _():
+            pl.semaphore_signal(barrier, 1, device_id={"head": hs, "seq": ss}, device_id_type=MESH)
 
     small = [pltpu.make_async_copy(src, dst, sems.at[FRAMES + n])
-             for n, (src, dst) in enumerate(((lists_hbm, lists), (counts_hbm, counts), (q_hbm, q_ref)))]
+             for n, (src, dst) in enumerate(((lists_hbm, lists), (counts_hbm, counts), (q_hbm, q)))]
 
     def loads(act):
         for fr in range(FRAMES):
@@ -310,112 +322,95 @@
     for cp in small:
         cp.wait()
 
-    def plan(i, e):
+    def plan(i, _):
         n = counts[0, frame * PER + i]
-
-        def chunk(g, e):
-            owner[e] = i
-            for u in range(G):
-                j = g * G + u
-                ids[e * G + u] = jnp.where(j < n, lists[i, j], NONE)
-            return e + 1
-
-        return lax.fori_loop(0, (n + G - 1) // G, chunk, e)
-
-    total = lax.fori_loop(0, PER, plan, jnp.int32(0))
-    owner[total] = 0
-    for u in range(G):
-        ids[total * G + u] = NONE
-    half = (total + 1) // 2
+        for j in range(MAXK):
+            ids[i * MAXK + j] = jnp.where(j < n, lists[j, frame * PER + i], NONE)
+        return 0
+
+    lax.fori_loop(0, PER, plan, 0)
     loads(lambda cp: cp.wait())
-
-    def pair(e):
-        return jnp.where(e < half, e, total), jnp.where(half + e < total, half + e, total)
-
+    pl.semaphore_wait(barrier, HEADS - self_home)
+
+    steps = MAXK // G
+    half = PER // 2
     blank = jnp.zeros((TILE, HD), bf16)
     ones = jnp.ones((16, TILE), bf16)
     none = jnp.zeros((16, TILE), bf16)
 
+    def tiles(t):
+        i = (hd + t + 1) % half
+        return i, i + half
+
     def score(e, s):
-        left, right = pair(e)
-        queries = jnp.concatenate([jnp.concatenate([q_ref[owner[left]], blank], 1),
-                                   jnp.concatenate([blank, q_ref[owner[right]]], 1)], 0)
-        keys = jnp.concatenate([jnp.concatenate([kv[ids[left * G + u], 0], kv[ids[right * G + u], 0]], 1)
+        left, right = tiles(e // steps)
+        g = (e % steps) * G
+        queries = jnp.concatenate([jnp.concatenate([q[left], blank], 1), jnp.concatenate([blank, q[right]], 1)], 0)
+        keys = jnp.concatenate([jnp.concatenate([kv[ids[left * MAXK + g + u], 0], kv[ids[right * MAXK + g + u], 0]], 1)
                                 for u in range(G)], 0)
         s[...] = lax.dot_general(keys, queries, (((1,), (1,)), ((), ())), preferred_element_type=f32)
 
     def weigh(e, s):
-        for side, chunk in enumerate(pair(e)):
+        g = (e % steps) * G
+        for side, i in enumerate(tiles(e // steps)):
             weights, values, live = [], [], []
             for u in range(G):
-                t = ids[chunk * G + u]
+                t = ids[i * MAXK + g + u]
                 part = s[u * TILE:(u + 1) * TILE, side * TILE:(side + 1) * TILE]
                 weights.append(jnp.exp2(part * SCALE).astype(bf16))
                 values.append(kv[t, 1])
                 live.append(jnp.where(t < NONE, ones, none))
             rows = jnp.concatenate([jnp.concatenate(values, 1), jnp.concatenate(live, 1)], 0)
-            acc[owner[chunk]] += lax.dot_general(rows, jnp.concatenate(weights, 0), (((1,), (0,)), ((), ())),
-                                                 preferred_element_type=f32)
+            acc[side] += lax.dot_general(rows, jnp.concatenate(weights, 0), (((1,), (0,)), ((), ())),
+                                         preferred_element_type=f32)
+
+    columns = out.at[:, pl.ds(pl.multiple_of(head * HD, HD), HD)]
+
+    def back(t, side, act):
+        i = tiles(t)[side]
+        slot = 2 * t + side
+        remote = (i != hd) | (frame != sq)
+
+        @pl.when(remote)
+        def _():
+            cp = pltpu.make_async_remote_copy(done.at[slot], columns, send.at[slot], recv.at[head],
+                                              device_id={"head": i, "seq": frame}, device_id_type=MESH)
+            cp.start() if act else cp.wait_send()
+
+        if act:
+            @pl.when(jnp.logical_not(remote))
+            def _():
+                pltpu.make_async_copy(done.at[slot], columns, recv.at[head]).start()
 
     score(jnp.int32(0), s0)
 
-    def body(h, _):
-        e = 2 * h
-        score(e + 1, s1)
-        weigh(e, s0)
-        score(e + 2, s0)
-        weigh(e + 1, s1)
+    def pair(t, _):
+        def body(h, _):
+            e = t * steps + 2 * h
+            score(e + 1, s1)
+            weigh(e, s0)
+            score(e + 2, s0)
+            weigh(e + 1, s1)
+            return 0
+
+        lax.fori_loop(0, steps // 2, body, 0)
+        for side in range(2):
+            done[2 * t + side] = jnp.transpose(acc[side, :HD] / acc[side, HD:HD + 1]).astype(bf16)
+            back(t, side, True)
+        acc[...] = jnp.zeros_like(acc)
         return 0
 
-    lax.fori_loop(0, (half + 1) // 2, body, 0)
-
-    def finish(i, _):
-        o_ref[i] = jnp.transpose(acc[i, :HD] / acc[i, HD:HD + 1]).astype(bf16)
-        return 0
-
-    lax.fori_loop(0, PER, finish, 0)
-
-
-def return_kernel(o_in, out, send, recv):
-    hd, sq, z, c, y, x, b, k = place()
-    frame = 4 * y + 2 * k + c
-    head = 2 * z + b
-    barrier = pltpu.get_barrier_semaphore()
-
-    def source(h):
-        return 2 * (h // 2) + x % 2, 4 * y + 2 * (h % 2) + x // 2
-
-    self_home = (frame == sq).astype(jnp.int32)
-    for h in range(HEADS):
-        hs, ss = source(h)
-
-        @pl.when((hs != hd) | (ss != sq))
-        def _():
-            pl.semaphore_signal(barrier, 1, device_id={"head": hs, "seq": ss}, device_id_type=MESH)
-    pl.semaphore_wait(barrier, HEADS - self_home)
-    columns = out.at[:, pl.ds(pl.multiple_of(head * HD, HD), HD)]
-
-    def copies(act):
-        for r in range(HEADS):
-            t = (hd + r) % HEADS
-            remote = (t != hd) | (frame != sq)
-
-            @pl.when(remote)
-            def _():
-                cp = pltpu.make_async_remote_copy(o_in.at[t], columns, send.at[r], recv.at[head],
-                                                  device_id={"head": t, "seq": frame}, device_id_type=MESH)
-                cp.start() if act else cp.wait_send()
-
-            if act:
-                @pl.when(jnp.logical_not(remote))
-                def _():
-                    pltpu.make_async_copy(o_in.at[t], columns, recv.at[head]).start()
-
-    copies(True)
+    lax.fori_loop(0, half, pair, 0)
     for h in range(HEADS):
         part = out.at[:, pl.ds(h * HD, HD)]
-        pltpu.make_async_copy(o_in.at[0], part, recv.at[h]).wait()
-    copies(False)
+        pltpu.make_async_copy(done.at[0], part, recv.at[h]).wait()
+
+    def sent(t, _):
+        back(t, 0, False)
+        back(t, 1, False)
+        return 0
+
+    lax.fori_loop(0, half, sent, 0)
 
 
 def local(projected, query_gain, key_gain, tile_lists, tile_counts):
@@ -429,7 +424,7 @@
     q, kv, _, lists, counts = pl.pallas_call(
         spread_kernel,
         out_shape=(sds((PER, TILE, HD), bf16), sds((FRAMES * PER, 2, TILE, HD), bf16), sds((PER, 2, TILE, HD), bf16),
-                   sds((PER, MAXK), jnp.int32), sds((1, FRAMES * PER), jnp.int32)),
+                   sds((MAXK, FRAMES * PER), jnp.int32), sds((1, FRAMES * PER), jnp.int32)),
         in_specs=[vmem] * 5 + [hbm] * 2,
         out_specs=(hbm,) * 5,
         scratch_shapes=[pltpu.VMEM((HEADS, 2, TILE, HD), bf16), pltpu.VMEM((HEADS, TILE, HD), bf16),
@@ -437,30 +432,20 @@
                         dma((2, 2, 4)), dma((2,)), dma((FRAMES, 4)), dma((FRAMES, 4)), dma((2,)), dma((2,))],
         compiler_params=pltpu.CompilerParams(collective_id=0, has_side_effects=True),
         name="spread",
-    )(jnp.transpose(projected, (1, 0, 2)), cosine, sine, query_gain[None], key_gain[None], tile_lists[0], tile_counts)
-    chunks = PER * (MAXK // G) + 1
-    attended = pl.pallas_call(
+    )(jnp.transpose(projected, (1, 0, 2)), cosine, sine, query_gain[None], key_gain[None], jnp.swapaxes(tile_lists, 1, 2)[0], tile_counts)
+    return pl.pallas_call(
         attend_kernel,
-        out_shape=sds((PER, TILE, HD), bf16),
+        out_shape=sds((TILE, HEADS * HD), bf16),
         in_specs=[hbm] * 4,
-        out_specs=vmem,
+        out_specs=hbm,
         scratch_shapes=[pltpu.VMEM((FRAMES * PER + 1, 2, TILE, HD), bf16), pltpu.VMEM((PER, TILE, HD), bf16),
-                        pltpu.SMEM((PER, MAXK), jnp.int32), pltpu.SMEM((1, FRAMES * PER), jnp.int32),
+                        pltpu.SMEM((MAXK, FRAMES * PER), jnp.int32), pltpu.SMEM((1, FRAMES * PER), jnp.int32),
                         pltpu.VMEM((G * TILE, 2 * TILE), f32), pltpu.VMEM((G * TILE, 2 * TILE), f32),
-                        pltpu.VMEM((PER, HD + 16, TILE), f32), pltpu.SMEM((chunks * G,), jnp.int32),
-                        pltpu.SMEM((chunks,), jnp.int32), dma((FRAMES + 3,))],
-        compiler_params=pltpu.CompilerParams(vmem_limit_bytes=40 * 1024 * 1024),
+                        pltpu.VMEM((2, HD + 16, TILE), f32), pltpu.SMEM((PER * MAXK,), jnp.int32),
+                        pltpu.VMEM((PER, TILE, HD), bf16), dma((FRAMES + 3,)), dma((PER,)), dma((HEADS,))],
+        compiler_params=pltpu.CompilerParams(collective_id=1, has_side_effects=True, vmem_limit_bytes=60 * 1024 * 1024),
         name="attend",
     )(lists, counts, q, kv)
-    return pl.pallas_call(
-        return_kernel,
-        out_shape=sds((TILE, HEADS * HD), bf16),
-        in_specs=[vmem],
-        out_specs=hbm,
-        scratch_shapes=[dma((HEADS,)), dma((HEADS,))],
-        compiler_params=pltpu.CompilerParams(collective_id=1, has_side_effects=True),
-        name="give_back",
-    )(attended)
 
 
 def solution(mesh):

time: 153 us -> 140 us (0.915)
  the two profiles are of different devices: /device:TPU:1 before, /device:TPU:15 now
where the time goes in v4:
time: 140 us; the launch traced here: 139 us
  Pallas kernels  134 us (96%)
  other arithmetic  3.15 us (2%)
  local copies, waits for them, and re-layouts  1.88 us (1%)
    pallas_call x1, Pallas kernels, local(): pl.pallas_call(spread_kernel, out_shape=(sds((PER, TILE, HD), bf16), sds(...  79.7 us
    pallas_call x1, Pallas kernels, local(): pl.pallas_call(attend_kernel, out_shape=sds((TILE, HEADS * HD), bf16), in...  54.3 us

profile of v4, /device:TPU:15, one launch (start us, length us, event | category | flops | bytes accessed | tf_op | source)
XLA Modules:
  0.0 139.1 jit_solution(11228555755236338708)
XLA Ops:
  0.0 0.7 multiply_bitcast_fusion
  0.7 0.7 convert_bitcast_fusion
  1.3 1.8 %sine_multiply_fusion = (f32[128,128]{1,0:T(8,128)}, f32[128,128]{1,0:T(8,128)}) fusion(f32[128,128]{1,0:T(8,128)} %constant.22.clone, f32[128]{0:T(128)} %constant.28, f32[128]{0:T(128)} %constant.27, f32[128]{0:T(128)S(1)} %convert_bitcast_fusion, f32[128]{0:T(128)S(1)} %multiply_bitcast_fusion), kind=kLoop, calls=%fused_computation | loop fusion | flops 65536 | bytes 198656 | tf_op jit(solution)/shard_map/mul | solution.py:47
  3.1 79.7 %spread.1 = (bf16[16,128,128]{2,1,0:T(8,128)(2,1)}, bf16[256,2,128,128]{3,2,1,0:T(8,128)(2,1)}, bf16[16,2,128,128]{3,2,1,0:T(8,128)(2,1)}, s32[96,256]{1,0:T(8,128)}, s32[1,256]{1,0:T(1,128)}) custom-call(bf16[3,128,2048]{2,1,0:T(8,128)(2,1)} %bitcast.10, f32[128,128]{1,0:T(8,128)} %get-tuple-element.14.cos, f32[128,128]{1,0:T(8,128)} %get-tuple-element.13.sin, ...), custom_call_target="tpu_custom_call" | custom-call | tf_op jit(solution)/shard_map/spread/pallas_call | solution.py:424
  82.9 54.3 %attend.1 = bf16[128,2048]{1,0:T(8,128)(2,1)} custom-call(s32[96,256]{1,0:T(8,128)} %get-tuple-element.9.lists_hbm, s32[1,256]{1,0:T(1,128)} %get-tuple-element.10.counts_hbm, bf16[16,128,128]{2,1,0:T(8,128)(2,1)} %get-tuple-element.11.q_hbm, bf16[256,2,128,128]{3,2,1,0:T(8,128)(2,1)} %get-tuple-element.12.kv_hbm), custom_call_target="tpu_custom_call" | custom-call | tf_op jit(solution)/shard_map/attend/pallas_call | solution.py:436
  137.2 1.9 %copy.12 = bf16[128,2048]{1,0:T(8,128)(2,1)} copy(bf16[128,2048]{1,0:T(8,128)(2,1)} %attend.1) | data formatting | bytes 1048576

commit v5 on v4

--- a/solution.py
+++ b/solution.py
@@ -28,23 +28,19 @@
 bf16 = jnp.bfloat16
 
 
-def rope_tables(sq, hd):
+def rope_rates():
     first = HD // 8
     second = (HD - first) // 2
-    rates = np.zeros((3, 1, HD), np.float32)
-    sign = np.ones((1, HD), np.float32)
+    rates = np.zeros((8, HD), np.float32)
+    rates[3] = 1.0
     offset = 0
     for axis, extent in enumerate((first, second, HD - first - second)):
         middle = extent // 2
         part = THETA ** (-2.0 * np.arange(middle) / extent)
-        rates[axis, 0, offset:offset + extent] = np.concatenate([part, part])
-        sign[0, offset:offset + middle] = -1.0
+        rates[axis, offset:offset + extent] = np.concatenate([part, part])
+        rates[3, offset:offset + middle] = -1.0
         offset += extent
-    token = np.arange(TILE)[:, None]
-    row = (hd * (TILE // GW) + token // GW).astype(f32)
-    column = (token % GW).astype(np.float32)
-    angles = sq.astype(f32) * rates[0] + row * rates[1] + column * rates[2]
-    return jnp.cos(angles), jnp.sin(angles) * sign
+    return rates
 
 
 def partner(field):
@@ -67,8 +63,8 @@
     return hd, sq, z, c, y, x, b, k
 
 
-def spread_kernel(proj, cos, sin, qg, kg, lists_in, counts_in, q, kv, transit, lists, counts,
-                  kv_in, q_in, sz, st, sq_sem, rz, rt, rq, s_mate, s_far, s_y, s_relay, s_cross, arrive, sl, rl):
+def spread_kernel(proj, rates, qg, kg, lists_in, counts_in, q, kv, transit, lists, counts,
+                  kv_in, q_in, cos, sin, sz, st, sq_sem, rz, rt, rq, s_mate, s_far, s_y, s_relay, s_cross, arrive, sl, rl):
     hd, sq, z, c, y, x, b, k = place()
     frame = 4 * y + 2 * k + c
     started = []
@@ -98,6 +94,12 @@
         @pl.when((t != hd) | (frame != sq))
         def _():
             pl.semaphore_signal(barrier, 1, device_id=dev(t, frame), device_id_type=MESH)
+    token = lax.broadcasted_iota(jnp.int32, (TILE, HD), 0)
+    row = (hd * (TILE // GW) + token // GW).astype(f32)
+    column = (token % GW).astype(f32)
+    angles = sq.astype(f32) * rates[0:1] + row * rates[1:2] + column * rates[2:3]
+    cos[...] = jnp.cos(angles)
+    sin[...] = jnp.sin(angles) * rates[3:4]
     self_home = (frame == sq).astype(jnp.int32)
     pl.semaphore_wait(barrier, HEADS - 1 + 4 + HEADS - self_home)
 
@@ -201,20 +203,19 @@
     lands = k == c
     relays = k != c
 
-    def from_here(fr, first, slot, m):
-        send((m == 0) | ((y < 3) & ((k == 0) | jnp.logical_not(first))),
+    def from_here(pred, fr, first, slot, m):
+        send(pred & ((m == 0) | ((y < 3) & ((k == 0) | jnp.logical_not(first)))),
              lambda: chunk(span(fr, m), fr, m, s_y.at[slot, 0, m], up))
-        send((m == 0) | ((y > 0) & ((k == 1) | first)),
+        send(pred & ((m == 0) | ((y > 0) & ((k == 1) | first))),
              lambda: chunk(span(fr, m), fr, m, s_y.at[slot, 1, m], down))
-        cross(True, fr, m)
-
-    def step_own(m):
+        cross(pred, fr, m)
+
+    def step_landing(m):
         @pl.when(lands)
         def _():
             for t in range(CH):
                 j = m * CH + t
                 pltpu.make_async_copy(kv.at[own * PER + j], kv.at[own * PER + j], rz.at[j]).wait()
-        arrived(relays, own, m)
         send(lands, lambda: chunk(span(own, m), own, m, s_mate.at[m], mate))
 
         @pl.when(lands)
@@ -223,12 +224,18 @@
                 j = m * CH + t
                 pltpu.make_async_copy(transit.at[j], transit.at[j], rt.at[j]).wait()
         send(lands, lambda: chunk(transit.at[pl.ds(m * CH, CH)], own, m, s_far.at[m], opposite))
-        from_here(own, b == 0, 0, m)
-
-    def step_guest(m):
-        arrived(True, guest, m)
+        from_here(lands, own, b == 0, 0, m)
+
+    def step_passing(m):
+        arrived(relays, guest, m)
         send(relays, lambda: chunk(span(guest, m), guest, m, s_mate.at[m], mate))
-        from_here(guest, b == 1, 1, m)
+        from_here(relays, guest, b == 1, 1, m)
+
+    def step_mate(pred, m):
+        arrived(pred & lands, guest, m)
+        from_here(pred & lands, guest, b == 1, 1, m)
+        arrived(pred & relays, own, m)
+        from_here(pred & relays, own, b == 0, 0, m)
 
     def step_rows(m):
         for first in (True, False):
@@ -245,18 +252,16 @@
 
     a, odd = z // 2, z % 2
     order = [a, (a + 3 + 2 * odd) % 4, (a + 1 + 2 * odd) % 4, (a + 2) % 4]
-    step_own(order[0])
-    step_own(order[1])
-    step_guest(order[0])
-    step_own(order[2])
-    step_guest(order[1])
-    step_rows(order[0])
-    step_own(order[3])
-    step_guest(order[2])
-    step_rows(order[1])
-    step_guest(order[3])
-    step_rows(order[2])
-    step_rows(order[3])
+    for n in range(4):
+        step_landing(order[n])
+        step_passing(order[n])
+        step_mate(relays, order[n])
+        if n >= 2:
+            step_mate(lands, order[n - 2])
+    step_mate(lands, order[2])
+    step_mate(lands, order[3])
+    for n in range(4):
+        step_rows(order[n])
     for second in range(2):
         fr = 4 * row_two + c + 2 * second
         arrived(True, fr, 0)
@@ -414,25 +419,22 @@
 
 
 def local(projected, query_gain, key_gain, tile_lists, tile_counts):
-    hd = lax.axis_index("head")
-    sq = lax.axis_index("seq")
     vmem = pl.BlockSpec(memory_space=pltpu.VMEM)
     hbm = pl.BlockSpec(memory_space=pltpu.HBM)
     sds = jax.ShapeDtypeStruct
     dma = pltpu.SemaphoreType.DMA
-    cosine, sine = rope_tables(sq, hd)
     q, kv, _, lists, counts = pl.pallas_call(
         spread_kernel,
         out_shape=(sds((PER, TILE, HD), bf16), sds((FRAMES * PER, 2, TILE, HD), bf16), sds((PER, 2, TILE, HD), bf16),
                    sds((MAXK, FRAMES * PER), jnp.int32), sds((1, FRAMES * PER), jnp.int32)),
-        in_specs=[vmem] * 5 + [hbm] * 2,
+        in_specs=[vmem] * 4 + [hbm] * 2,
         out_specs=(hbm,) * 5,
         scratch_shapes=[pltpu.VMEM((HEADS, 2, TILE, HD), bf16), pltpu.VMEM((HEADS, TILE, HD), bf16),
-                        dma((8,)), dma((8,)), dma((16,)), dma((16,)), dma((16,)), dma((16,)), dma((4,)), dma((4,)),
+                        pltpu.VMEM((TILE, HD), f32), pltpu.VMEM((TILE, HD), f32), dma((8,)), dma((8,)), dma((16,)), dma((16,)), dma((16,)), dma((16,)), dma((4,)), dma((4,)),
                         dma((2, 2, 4)), dma((2,)), dma((FRAMES, 4)), dma((FRAMES, 4)), dma((2,)), dma((2,))],
         compiler_params=pltpu.CompilerParams(collective_id=0, has_side_effects=True),
         name="spread",
-    )(jnp.transpose(projected, (1, 0, 2)), cosine, sine, query_gain[None], key_gain[None], jnp.swapaxes(tile_lists, 1, 2)[0], tile_counts)
+    )(jnp.transpose(projected, (1, 0, 2)), rope_rates(), query_gain[None], key_gain[None], jnp.swapaxes(tile_lists, 1, 2)[0], tile_counts)
     return pl.pallas_call(
         attend_kernel,
         out_shape=sds((TILE, HEADS * HD), bf16),

time: 140 us -> 129 us (0.921)
  Pallas kernels: 134 us -> 127 us
  other arithmetic: 3.15 us -> 0 us
    pallas_call x1, Pallas kernels: 54.3 us -> 49 us  [local(): pl.pallas_call(attend_kernel, out_shape=sds((TILE, HEADS * HD), bf16), in...]
    mul x2 -> x0, other arithmetic: 2.49 us -> none  [the longest x1 1.83 us: rope_tables(): return (jnp.cos(angles), jnp.sin(angles) * sign)]
    pallas_call x1, Pallas kernels: 79.7 us -> 78.3 us  [local(): pl.pallas_call(spread_kernel, out_shape=(sds((PER, TILE, HD), bf16), sds(...]
where the time goes in v5:
time: 129 us
  Pallas kernels  127 us (98%)
  local copies, waits for them, and re-layouts  1.88 us (1%)
    pallas_call x1, Pallas kernels, local(): pl.pallas_call(spread_kernel, out_shape=(sds((PER, TILE, HD), bf16), sds(...  78.3 us
    pallas_call x1, Pallas kernels, local(): pl.pallas_call(attend_kernel, out_shape=sds((TILE, HEADS * HD), bf16), in...  49 us

profile of v5, /device:TPU:15, one launch (start us, length us, event | category | flops | bytes accessed | tf_op | source)
XLA Modules:
  0.0 129.2 jit_solution(12467017235700801203)
XLA Ops:
  0.0 78.3 %spread.1 = (bf16[16,128,128]{2,1,0:T(8,128)(2,1)}, bf16[256,2,128,128]{3,2,1,0:T(8,128)(2,1)}, bf16[16,2,128,128]{3,2,1,0:T(8,128)(2,1)}, s32[96,256]{1,0:T(8,128)}, s32[1,256]{1,0:T(1,128)}) custom-call(bf16[3,128,2048]{2,1,0:T(8,128)(2,1)} %bitcast.6, f32[8,128]{1,0:T(8,128)} %constant.2.clone.rates, f32[1,128]{1,0:T(1,128)} %bitcast.8, ...), custom_call_target="tpu_custom_call" | custom-call | tf_op jit(solution)/shard_map/spread/pallas_call | solution.py:426
  78.3 49.0 %attend.1 = bf16[128,2048]{1,0:T(8,128)(2,1)} custom-call(s32[96,256]{1,0:T(8,128)} %get-tuple-element.9.lists_hbm, s32[1,256]{1,0:T(1,128)} %get-tuple-element.10.counts_hbm, bf16[16,128,128]{2,1,0:T(8,128)(2,1)} %get-tuple-element.11.q_hbm, bf16[256,2,128,128]{3,2,1,0:T(8,128)(2,1)} %get-tuple-element.12.kv_hbm), custom_call_target="tpu_custom_call" | custom-call | tf_op jit(solution)/shard_map/attend/pallas_call | solution.py:438
  127.3 1.9 %copy.8 = bf16[128,2048]{1,0:T(8,128)(2,1)} copy(bf16[128,2048]{1,0:T(8,128)(2,1)} %attend.1) | data formatting | bytes 1048576

commit v6 on v5

--- a/solution.py
+++ b/solution.py
@@ -63,8 +63,9 @@
     return hd, sq, z, c, y, x, b, k
 
 
-def spread_kernel(proj, rates, qg, kg, lists_in, counts_in, q, kv, transit, lists, counts,
-                  kv_in, q_in, cos, sin, sz, st, sq_sem, rz, rt, rq, s_mate, s_far, s_y, s_relay, s_cross, arrive, sl, rl):
+def attend_kernel(proj, rates, qg, kg, lists_in, counts_in, out, lists, counts,
+                  kv, q, transit, kv_in, q_in, cos, sin, lists_s, counts_s, ids, s0, s1, acc, done,
+                  sz, st, sq_sem, rz, rt, rq, s_mate, s_far, s_y, s_relay, s_cross, arrive, sl, rl, s_back, r_back):
     hd, sq, z, c, y, x, b, k = place()
     frame = 4 * y + 2 * k + c
     started = []
@@ -94,6 +95,12 @@
         @pl.when((t != hd) | (frame != sq))
         def _():
             pl.semaphore_signal(barrier, 1, device_id=dev(t, frame), device_id_type=MESH)
+    for h in range(HEADS):
+        hs, ss = 2 * (h // 2) + k, 4 * y + 2 * (h % 2) + b
+
+        @pl.when((hs != hd) | (ss != sq))
+        def _():
+            pl.semaphore_signal(barrier, 1, device_id=dev(hs, ss), device_id_type=MESH)
     token = lax.broadcasted_iota(jnp.int32, (TILE, HD), 0)
     row = (hd * (TILE // GW) + token // GW).astype(f32)
     column = (token % GW).astype(f32)
@@ -101,7 +108,18 @@
     cos[...] = jnp.cos(angles)
     sin[...] = jnp.sin(angles) * rates[3:4]
     self_home = (frame == sq).astype(jnp.int32)
-    pl.semaphore_wait(barrier, HEADS - 1 + 4 + HEADS - self_home)
+    pl.semaphore_wait(barrier, HEADS - 1 + 4 + 2 * (HEADS - self_home))
+
+    mine = b == c
+    send(mine, lambda: pltpu.make_async_remote_copy(lists_in, lists, sl.at[0], rl.at[0],
+                                                    device_id=sibling, device_id_type=MESH))
+    send(mine, lambda: pltpu.make_async_remote_copy(counts_in, counts, sl.at[1], rl.at[1],
+                                                    device_id=sibling, device_id_type=MESH))
+
+    @pl.when(mine)
+    def _():
+        pltpu.make_async_copy(lists_in, lists, rl.at[0]).start()
+        pltpu.make_async_copy(counts_in, counts, rl.at[1]).start()
 
     def line(src, dst, send_sem, recv_sem, target, seq, act):
         remote = (target != hd) | (seq != sq)
@@ -156,16 +174,23 @@
     each(line_kv, True)
     each(line_q, True)
 
-    mine = b == c
-    send(mine, lambda: pltpu.make_async_remote_copy(lists_in, lists, sl.at[0], rl.at[0],
-                                                    device_id=sibling, device_id_type=MESH))
-    send(mine, lambda: pltpu.make_async_remote_copy(counts_in, counts, sl.at[1], rl.at[1],
-                                                    device_id=sibling, device_id_type=MESH))
-
-    @pl.when(mine)
-    def _():
-        pltpu.make_async_copy(lists_in, lists, rl.at[0]).start()
-        pltpu.make_async_copy(counts_in, counts, rl.at[1]).start()
+    pltpu.make_async_copy(lists_in, lists, rl.at[0]).wait()
+    pltpu.make_async_copy(counts_in, counts, rl.at[1]).wait()
+    fetch = [pltpu.make_async_copy(lists, lists_s, rl.at[2]), pltpu.make_async_copy(counts, counts_s, rl.at[3])]
+    for cp in fetch:
+        cp.start()
+    for cp in fetch:
+        cp.wait()
+
+    def plan(i, _):
+        n = counts_s[0, frame * PER + i]
+        for j in range(MAXK):
+            ids[i * MAXK + j] = jnp.where(j < n, lists_s[j, frame * PER + i], NONE)
+        return 0
+
+    lax.fori_loop(0, PER, plan, 0)
+    acc[...] = jnp.zeros_like(acc)
+    kv[NONE] = jnp.zeros((2, TILE, HD), bf16)
 
     def span(fr, m):
         return kv.at[pl.ds(fr * PER + m * CH, CH)]
@@ -269,8 +294,6 @@
 
     for j in range(PER):
         pltpu.make_async_copy(q.at[j], q.at[j], rq.at[j]).wait()
-    pltpu.make_async_copy(lists_in, lists, rl.at[0]).wait()
-    pltpu.make_async_copy(counts_in, counts, rl.at[1]).wait()
     for m in range(4):
         for first in (True, False):
             lane = 1 - c + (0 if first else 2)
@@ -279,63 +302,6 @@
             arrived(up_crosses(first, m, 1 - c), 4 * row_up + lane, m)
             if m == 0:
                 arrived(True, 4 * row_two + lane, m)
-    for pred, make in started:
-        @pl.when(pred)
-        def _():
-            make().wait_send()
-    each(line_kv, False)
-    each(line_q, False)
-
-
-def attend_kernel(lists_hbm, counts_hbm, q_hbm, kv_hbm, out, kv, q, lists, counts, s0, s1, acc, ids, done, sems,
-                  send, recv):
-    hd, sq, z, c, y, x, b, k = place()
-    frame = 4 * y + 2 * k + c
-    head = 2 * z + b
-
-    barrier = pltpu.get_barrier_semaphore()
-    self_home = (frame == sq).astype(jnp.int32)
-    for h in range(HEADS):
-        hs, ss = 2 * (h // 2) + k, 4 * y + 2 * (h % 2) + b
-
-        @pl.when((hs != hd) | (ss != sq))
-        def _():
-            pl.semaphore_signal(barrier, 1, device_id={"head": hs, "seq": ss}, device_id_type=MESH)
-
-    small = [pltpu.make_async_copy(src, dst, sems.at[FRAMES + n])
-             for n, (src, dst) in enumerate(((lists_hbm, lists), (counts_hbm, counts), (q_hbm, q)))]
-
-    def loads(act):
-        for fr in range(FRAMES):
-            near = jnp.abs(fr - frame) <= 4
-
-            @pl.when(near)
-            def _():
-                part = pl.ds(fr * PER, PER)
-                act(pltpu.make_async_copy(kv_hbm.at[part], kv.at[part], sems.at[fr]))
-
-            @pl.when(jnp.logical_not(near))
-            def _():
-                part = pl.ds(fr * PER, CH)
-                act(pltpu.make_async_copy(kv_hbm.at[part], kv.at[part], sems.at[fr]))
-
-    for cp in small:
-        cp.start()
-    loads(lambda cp: cp.start())
-    acc[...] = jnp.zeros_like(acc)
-    kv[NONE] = jnp.zeros((2, TILE, HD), bf16)
-    for cp in small:
-        cp.wait()
-
-    def plan(i, _):
-        n = counts[0, frame * PER + i]
-        for j in range(MAXK):
-            ids[i * MAXK + j] = jnp.where(j < n, lists[j, frame * PER + i], NONE)
-        return 0
-
-    lax.fori_loop(0, PER, plan, 0)
-    loads(lambda cp: cp.wait())
-    pl.semaphore_wait(barrier, HEADS - self_home)
 
     steps = MAXK // G
     half = PER // 2
@@ -369,6 +335,7 @@
             acc[side] += lax.dot_general(rows, jnp.concatenate(weights, 0), (((1,), (0,)), ((), ())),
                                          preferred_element_type=f32)
 
+    head = 2 * z + b
     columns = out.at[:, pl.ds(pl.multiple_of(head * HD, HD), HD)]
 
     def back(t, side, act):
@@ -378,14 +345,14 @@
 
         @pl.when(remote)
         def _():
-            cp = pltpu.make_async_remote_copy(done.at[slot], columns, send.at[slot], recv.at[head],
+            cp = pltpu.make_async_remote_copy(done.at[slot], columns, s_back.at[slot], r_back.at[head],
                                               device_id={"head": i, "seq": frame}, device_id_type=MESH)
             cp.start() if act else cp.wait_send()
 
         if act:
             @pl.when(jnp.logical_not(remote))
             def _():
-                pltpu.make_async_copy(done.at[slot], columns, recv.at[head]).start()
+                pltpu.make_async_copy(done.at[slot], columns, r_back.at[head]).start()
 
     score(jnp.int32(0), s0)
 
@@ -408,7 +375,7 @@
     lax.fori_loop(0, half, pair, 0)
     for h in range(HEADS):
         part = out.at[:, pl.ds(h * HD, HD)]
-        pltpu.make_async_copy(done.at[0], part, recv.at[h]).wait()
+        pltpu.make_async_copy(done.at[0], part, r_back.at[h]).wait()
 
     def sent(t, _):
         back(t, 0, False)
@@ -416,6 +383,12 @@
         return 0
 
     lax.fori_loop(0, half, sent, 0)
+    for pred, make in started:
+        @pl.when(pred)
+        def _():
+            make().wait_send()
+    each(line_kv, False)
+    each(line_q, False)
 
 
 def local(projected, query_gain, key_gain, tile_lists, tile_counts):
@@ -423,31 +396,27 @@
     hbm = pl.BlockSpec(memory_space=pltpu.HBM)
     sds = jax.ShapeDtypeStruct
     dma = pltpu.SemaphoreType.DMA
-    q, kv, _, lists, counts = pl.pallas_call(
-        spread_kernel,
-        out_shape=(sds((PER, TILE, HD), bf16), sds((FRAMES * PER, 2, TILE, HD), bf16), sds((PER, 2, TILE, HD), bf16),
-                   sds((MAXK, FRAMES * PER), jnp.int32), sds((1, FRAMES * PER), jnp.int32)),
+    out, _, _ = pl.pallas_call(
+        attend_kernel,
+        out_shape=(sds((TILE, HEADS * HD), bf16), sds((MAXK, FRAMES * PER), jnp.int32),
+                   sds((1, FRAMES * PER), jnp.int32)),
         in_specs=[vmem] * 4 + [hbm] * 2,
-        out_specs=(hbm,) * 5,
-        scratch_shapes=[pltpu.VMEM((HEADS, 2, TILE, HD), bf16), pltpu.VMEM((HEADS, TILE, HD), bf16),
-                        pltpu.VMEM((TILE, HD), f32), pltpu.VMEM((TILE, HD), f32), dma((8,)), dma((8,)), dma((16,)), dma((16,)), dma((16,)), dma((16,)), dma((4,)), dma((4,)),
-                        dma((2, 2, 4)), dma((2,)), dma((FRAMES, 4)), dma((FRAMES, 4)), dma((2,)), dma((2,))],
-        compiler_params=pltpu.CompilerParams(collective_id=0, has_side_effects=True),
-        name="spread",
-    )(jnp.transpose(projected, (1, 0, 2)), rope_rates(), query_gain[None], key_gain[None], jnp.swapaxes(tile_lists, 1, 2)[0], tile_counts)
-    return pl.pallas_call(
-        attend_kernel,
-        out_shape=sds((TILE, HEADS * HD), bf16),
-        in_specs=[hbm] * 4,
-        out_specs=hbm,
+        out_specs=(hbm,) * 3,
         scratch_shapes=[pltpu.VMEM((FRAMES * PER + 1, 2, TILE, HD), bf16), pltpu.VMEM((PER, TILE, HD), bf16),
+                        pltpu.VMEM((PER, 2, TILE, HD), bf16), pltpu.VMEM((HEADS, 2, TILE, HD), bf16),
+                        pltpu.VMEM((HEADS, TILE, HD), bf16), pltpu.VMEM((TILE, HD), f32), pltpu.VMEM((TILE, HD), f32),
                         pltpu.SMEM((MAXK, FRAMES * PER), jnp.int32), pltpu.SMEM((1, FRAMES * PER), jnp.int32),
+                        pltpu.SMEM((PER * MAXK,), jnp.int32),
                         pltpu.VMEM((G * TILE, 2 * TILE), f32), pltpu.VMEM((G * TILE, 2 * TILE), f32),
-                        pltpu.VMEM((2, HD + 16, TILE), f32), pltpu.SMEM((PER * MAXK,), jnp.int32),
-                        pltpu.VMEM((PER, TILE, HD), bf16), dma((FRAMES + 3,)), dma((PER,)), dma((HEADS,))],
-        compiler_params=pltpu.CompilerParams(collective_id=1, has_side_effects=True, vmem_limit_bytes=60 * 1024 * 1024),
+                        pltpu.VMEM((2, HD + 16, TILE), f32), pltpu.VMEM((PER, TILE, HD), bf16),
+                        dma((8,)), dma((8,)), dma((16,)), dma((16,)), dma((16,)), dma((16,)), dma((4,)), dma((4,)),
+                        dma((2, 2, 4)), dma((2,)), dma((FRAMES, 4)), dma((FRAMES, 4)), dma((2,)), dma((4,)),
+                        dma((PER,)), dma((HEADS,))],
+        compiler_params=pltpu.CompilerParams(collective_id=0, has_side_effects=True, vmem_limit_bytes=60 * 1024 * 1024),
         name="attend",
-    )(lists, counts, q, kv)
+    )(jnp.transpose(projected, (1, 0, 2)), rope_rates(), query_gain[None], key_gain[None],
+      jnp.swapaxes(tile_lists, 1, 2)[0], tile_counts)
+    return out
 
 
 def solution(mesh):

time: 129 us -> 125 us (0.969)
  Pallas kernels: 127 us -> 123 us
    pallas_call x2 -> x1, Pallas kernels: 127 us -> 123 us  [local(): pl.pallas_call(attend_kernel, out_shape=(sds((TILE, HEADS * HD), bf16), s...]
where the time goes in v6:
time: 125 us
  Pallas kernels  123 us (98%)
  local copies, waits for them, and re-layouts  1.88 us (2%)
    pallas_call x1, Pallas kernels, local(): pl.pallas_call(attend_kernel, out_shape=(sds((TILE, HEADS * HD), bf16), s...  123 us

profile of v6, /device:TPU:15, one launch (start us, length us, event | category | flops | bytes accessed | tf_op | source)
XLA Modules:
  0.0 124.9 jit_solution(17718908725518089219)
XLA Ops:
  0.0 123.0 %attend.1 = (bf16[128,2048]{1,0:T(8,128)(2,1)}, s32[96,256]{1,0:T(8,128)}, s32[1,256]{1,0:T(1,128)}) custom-call(bf16[3,128,2048]{2,1,0:T(8,128)(2,1)} %bitcast.6, f32[8,128]{1,0:T(8,128)} %constant.2.clone.rates, f32[1,128]{1,0:T(1,128)} %bitcast.8, f32[1,128]{1,0:T(1,128)} %bitcast.9, s32[96,256]{1,0:T(8,128)} %bitcast.7, s32[1,256]{1,0:T(1,128)} %counts_in.1), custom_call_target="tpu_custom_call" | custom-call | tf_op jit(solution)/shard_map/attend/pallas_call | solution.py:399
  123.0 1.9 %copy.8 = bf16[128,2048]{1,0:T(8,128)(2,1)} copy(bf16[128,2048]{1,0:T(8,128)(2,1)} %get-tuple-element.6) | data formatting | bytes 1048576

commit v7 on v6

--- a/solution.py
+++ b/solution.py
@@ -20,7 +20,7 @@
 MAXK = 96
 THETA = 256.0
 SCALE = math.log2(math.e) / math.sqrt(HD)
-G = 16
+G = 48
 NONE = FRAMES * PER
 
 MESH = pl.DeviceIdType.MESH
@@ -172,25 +172,6 @@
         lax.fori_loop(0, 8, body, 0)
 
     each(line_kv, True)
-    each(line_q, True)
-
-    pltpu.make_async_copy(lists_in, lists, rl.at[0]).wait()
-    pltpu.make_async_copy(counts_in, counts, rl.at[1]).wait()
-    fetch = [pltpu.make_async_copy(lists, lists_s, rl.at[2]), pltpu.make_async_copy(counts, counts_s, rl.at[3])]
-    for cp in fetch:
-        cp.start()
-    for cp in fetch:
-        cp.wait()
-
-    def plan(i, _):
-        n = counts_s[0, frame * PER + i]
-        for j in range(MAXK):
-            ids[i * MAXK + j] = jnp.where(j < n, lists_s[j, frame * PER + i], NONE)
-        return 0
-
-    lax.fori_loop(0, PER, plan, 0)
-    acc[...] = jnp.zeros_like(acc)
-    kv[NONE] = jnp.zeros((2, TILE, HD), bf16)
 
     def span(fr, m):
         return kv.at[pl.ds(fr * PER + m * CH, CH)]
@@ -277,10 +258,33 @@
 
     a, odd = z // 2, z % 2
     order = [a, (a + 3 + 2 * odd) % 4, (a + 1 + 2 * odd) % 4, (a + 2) % 4]
+    def make_plan():
+        pltpu.make_async_copy(lists_in, lists, rl.at[0]).wait()
+        pltpu.make_async_copy(counts_in, counts, rl.at[1]).wait()
+        fetch = [pltpu.make_async_copy(lists, lists_s, rl.at[2]), pltpu.make_async_copy(counts, counts_s, rl.at[3])]
+        for cp in fetch:
+            cp.start()
+        for cp in fetch:
+            cp.wait()
+
+        def plan(i, _):
+            n = counts_s[0, frame * PER + i]
+            for j in range(MAXK):
+                ids[i * MAXK + j] = jnp.where(j < n, lists_s[j, frame * PER + i], NONE)
+            return 0
+
+        lax.fori_loop(0, PER, plan, 0)
+        acc[...] = jnp.zeros_like(acc)
+        kv[NONE] = jnp.zeros((2, TILE, HD), bf16)
+
     for n in range(4):
         step_landing(order[n])
         step_passing(order[n])
         step_mate(relays, order[n])
+        if n == 0:
+            each(line_q, True)
+        if n == 1:
+            make_plan()
         if n >= 2:
             step_mate(lands, order[n - 2])
     step_mate(lands, order[2])

time: 125 us -> 118 us (0.944)
  Pallas kernels: 123 us -> 116 us
    pallas_call x1, Pallas kernels: 123 us -> 116 us  [local(): pl.pallas_call(attend_kernel, out_shape=(sds((TILE, HEADS * HD), bf16), s...]
where the time goes in v7:
time: 118 us
  Pallas kernels  116 us (98%)
  local copies, waits for them, and re-layouts  1.88 us (2%)
    pallas_call x1, Pallas kernels, local(): pl.pallas_call(attend_kernel, out_shape=(sds((TILE, HEADS * HD), bf16), s...  116 us

profile of v7, /device:TPU:15, one launch (start us, length us, event | category | flops | bytes accessed | tf_op | source)
XLA Modules:
  0.0 118.1 jit_solution(8623841735871521379)
XLA Ops:
  0.0 116.2 %attend.1 = (bf16[128,2048]{1,0:T(8,128)(2,1)}, s32[96,256]{1,0:T(8,128)}, s32[1,256]{1,0:T(1,128)}) custom-call(bf16[3,128,2048]{2,1,0:T(8,128)(2,1)} %bitcast.6, f32[8,128]{1,0:T(8,128)} %constant.2.clone.rates, f32[1,128]{1,0:T(1,128)} %bitcast.8, f32[1,128]{1,0:T(1,128)} %bitcast.9, s32[96,256]{1,0:T(8,128)} %bitcast.7, s32[1,256]{1,0:T(1,128)} %counts_in.1), custom_call_target="tpu_custom_call" | custom-call | tf_op jit(solution)/shard_map/attend/pallas_call | solution.py:403
  116.2 1.9 %copy.8 = bf16[128,2048]{1,0:T(8,128)(2,1)} copy(bf16[128,2048]{1,0:T(8,128)(2,1)} %get-tuple-element.6) | data formatting | bytes 1048576

commit v8 on v7

--- a/solution.py
+++ b/solution.py
@@ -287,10 +287,12 @@
             make_plan()
         if n >= 2:
             step_mate(lands, order[n - 2])
+    step_rows(order[0])
     step_mate(lands, order[2])
+    step_rows(order[1])
     step_mate(lands, order[3])
-    for n in range(4):
-        step_rows(order[n])
+    step_rows(order[2])
+    step_rows(order[3])
     for second in range(2):
         fr = 4 * row_two + c + 2 * second
         arrived(True, fr, 0)

time: 118 us -> 118 us (level)
  no operation moved by 1% of the time
where the time goes in v8:
time: 118 us
  Pallas kernels  116 us (98%)
  local copies, waits for them, and re-layouts  1.88 us (2%)
    pallas_call x1, Pallas kernels, local(): pl.pallas_call(attend_kernel, out_shape=(sds((TILE, HEADS * HD), bf16), s...  116 us

profile of v8, /device:TPU:15, one launch (start us, length us, event | category | flops | bytes accessed | tf_op | source)
XLA Modules:
  0.0 118.1 jit_solution(12979779873987884441)
XLA Ops:
  0.0 116.2 %attend.1 = (bf16[128,2048]{1,0:T(8,128)(2,1)}, s32[96,256]{1,0:T(8,128)}, s32[1,256]{1,0:T(1,128)}) custom-call(bf16[3,128,2048]{2,1,0:T(8,128)(2,1)} %bitcast.6, f32[8,128]{1,0:T(8,128)} %constant.2.clone.rates, f32[1,128]{1,0:T(1,128)} %bitcast.8, f32[1,128]{1,0:T(1,128)} %bitcast.9, s32[96,256]{1,0:T(8,128)} %bitcast.7, s32[1,256]{1,0:T(1,128)} %counts_in.1), custom_call_target="tpu_custom_call" | custom-call | tf_op jit(solution)/shard_map/attend/pallas_call | solution.py:405
  116.2 1.9 %copy.8 = bf16[128,2048]{1,0:T(8,128)(2,1)} copy(bf16[128,2048]{1,0:T(8,128)(2,1)} %get-tuple-element.6) | data formatting | bytes 1048576
